TPU v7x, 32 devices: a whole 2x2x4 slice. The times are simulated.
32 devices in a mesh: section: 2 (over core), seq: 4 (over z), head: 4 (over y, x).
Axes of the slice: x: 2, y: 2, z: 4, core: 2. Of those that a mesh axis runs over, the one named last changes fastest.
Arguments:
- section_ends: float32 [2, 2, 4, 4096, 1024], P('section', None, 'seq', 'head'), may hold values from -6 to 6
- norm_gain: float32 [2, 1024], P('section'), may hold values from 0.1 to 1.9
- in_weight: float32 [2, 1024, 4384], P('section', ('seq', 'head')), may hold values from -0.1875 to 0.1875
- conv_weight: float32 [2, 4, 2304], P('section'), may hold values from -3 to 3
- conv_bias: float32 [2, 2304], P('section'), may hold values from -1.2 to 1.2
- dt_bias: float32 [2, 32], P('section'), may hold values from -6 to -2.5
- a_log: float32 [2, 32], P('section'), may hold values from 0 to 2.77
- skip_gain: float32 [2, 32], P('section'), may hold values from 0.5 to 1.5
- gated_gain: float32 [2, 2048], P('section'), may hold values from 0.1 to 1.9
- out_weight: float32 [2, 2048, 1024], P('section', ('seq', 'head')), may hold values from -0.125 to 0.125
Outputs:
- ends_out: float32 [2, 2, 4, 4096, 1024], P('section', None, 'seq', 'head')
- norm_gain_grad: float32 [2, 1024], P('section')
- in_weight_grad: float32 [2, 1024, 4384], P('section', ('seq', 'head'))
- conv_weight_grad: float32 [2, 4, 2304], P('section')
- conv_bias_grad: float32 [2, 2304], P('section')
- dt_bias_grad: float32 [2, 32], P('section')
- a_log_grad: float32 [2, 32], P('section')
- skip_grad: float32 [2, 32], P('section')
- gated_gain_grad: float32 [2, 2048], P('section')
- out_weight_grad: float32 [2, 2048, 1024], P('section', ('seq', 'head'))
All inputs are finite; a program needn't handle non-finite values.
Results may differ from a plain program's by a relative error of at most 0.017.
The roundings to bfloat16 on the way count: a program that leaves them out, or rounds other values in their place, can miss the bound.
Values may be sent and summed in bfloat16 or wider, within the bound.
No kernel may reach another device: no remote copies, remote signals or barrier semaphores. Data moves between devices by JAX's collectives and lax.ppermute only.
A program may use at most 768 MiB of HBM per device.

v0:
```python
import functools

import jax
import jax.numpy as jnp
from jax import lax
from jax.experimental import pallas as pl
from jax.experimental.pallas import tpu as pltpu
from jax.sharding import PartitionSpec as P

BLOCK = 128
GROUP = 4
SUBS = 2
EPSILON = 1e-05
LOG2E = 1.4426950408889634
HIGHEST = lax.Precision.HIGHEST
F32 = jnp.float32
LOW = jnp.bfloat16
VMEM_BYTES = 56 * 1024 * 1024


def contract(a, b, a_dim, b_dim, precision=None):
    return lax.dot_general(
        a, b, (((a_dim,), (b_dim,)), ((), ())), preferred_element_type=F32, precision=precision
    )


def sigmoid(v):
    return 0.5 * jnp.tanh(0.5 * v) + 0.5


def softplus(v):
    return jnp.maximum(v, 0.0) + jnp.log1p(jnp.exp(-jnp.abs(v)))


def ordered(transposed=False):
    row = lax.broadcasted_iota(jnp.int32, (BLOCK, BLOCK), 0)
    col = lax.broadcasted_iota(jnp.int32, (BLOCK, BLOCK), 1)
    return (row >= col) if transposed else (row <= col)


def fold(values):
    return jnp.sum(values.reshape(values.shape[0] // 8, 8, values.shape[1]), axis=0)


def column_sum(values):
    return jnp.sum(values, axis=0, keepdims=True)


def grouped(heads, width, body, unroll=8):
    size = GROUP if heads % GROUP == 0 else 1

    def step(g, carry):
        first = g * size
        rows = pl.ds(pl.multiple_of(first * width, size * width), size * width)
        parts = [(pl.ds(first + i, 1), slice(i * width, (i + 1) * width)) for i in range(size)]
        body(first, rows, parts)
        return carry

    lax.fori_loop(0, heads // size, step, 0, unroll=min(unroll, heads // size))


def spread_lanes(columns, place, target):
    target[...] = jnp.broadcast_to(columns[:, place : place + 1], target.shape)


def call(kernel, grid, ins, outs, scratch, flops, nbytes, transcendentals=0):
    arrays = [a for a, _ in ins]
    return pl.pallas_call(
        kernel,
        grid=grid,
        in_specs=[s for _, s in ins],
        out_specs=[s for _, s in outs],
        out_shape=[a for a, _ in outs],
        scratch_shapes=scratch,
        compiler_params=pltpu.CompilerParams(
            dimension_semantics=("arbitrary",) * len(grid), vmem_limit_bytes=VMEM_BYTES
        ),
        cost_estimate=pl.CostEstimate(
            flops=flops, bytes_accessed=nbytes, transcendentals=transcendentals
        ),
    )(*arrays)


def whole(array):
    rank = len(array.shape)
    return (
        array, pl.BlockSpec(array.shape, lambda b: (0,) * rank, pipeline_mode=pl.Buffered(1))
    )


def out(shape, dtype):
    return jax.ShapeDtypeStruct(shape, dtype)


def tokens(array, place=lambda b: b, rows=None, at=0):
    rows = array.shape[0] if rows is None else rows
    return (array, pl.BlockSpec((rows, BLOCK), lambda b: (at, place(b))))


def token_out(rows, length, dtype, place=lambda b: b):
    return (out((rows, length), dtype), pl.BlockSpec((rows, BLOCK), lambda b: (0, place(b))))


def fixed_out(shape, dtype):
    return (out(shape, dtype), pl.BlockSpec(shape, lambda b: (0,) * len(shape)))


def states_kernel(
    u_ref, halo_ref, step_ref, chan_ref, bias_ref, rate_ref,
    xs_ref, slope_ref, bc_ref, dt_ref, w_ref, wt_ref, wcol_ref, sin_ref, send_ref,
    tail, state, scale, ewend, offset, cw_ref, cb_ref,
):
    step = pl.program_id(0)
    heads = step_ref.shape[0]
    inner = xs_ref.shape[0]
    width = inner // heads
    taps = cw_ref.shape[0]
    n_state = bc_ref.shape[0] // 2

    @pl.when(step == 0)
    def _():
        for k in range(taps):
            spread_lanes(chan_ref, k, cw_ref.at[k])
        spread_lanes(chan_ref, taps, cb_ref)
        for k in range(taps - 1):
            tail[k] = pltpu.roll(halo_ref[...].astype(F32), taps - 1 - k, 1)
        state[...] = jnp.zeros_like(state)
        offset[...] = jnp.zeros_like(offset)

    dt = softplus(step_ref[...].astype(F32) + bias_ref[...])
    loga = dt * rate_ref[...]
    w = contract(loga, ordered().astype(F32), 1, 0, HIGHEST)
    wcol_ref[...] = contract(ordered(True).astype(F32), loga, 1, 1, HIGHEST)
    wend = jnp.broadcast_to(w[:, BLOCK - 1 :], w.shape)
    dt_ref[...] = dt
    w_ref[...] = w
    wt_ref[...] = w + offset[...]
    offset[...] += wend
    scale[...] = dt * jnp.exp(wend - w)
    ewend[...] = jnp.exp(wend)

    def conv(rows):
        u = u_ref[rows, :].astype(F32)
        lane = lax.broadcasted_iota(jnp.int32, (1, BLOCK), 1)
        c = cb_ref[rows, :] + cw_ref[taps - 1, rows, :] * u
        for k in range(taps - 1):
            back = taps - 1 - k
            rolled = pltpu.roll(u, back, 1)
            c = c + cw_ref[k, rows, :] * jnp.where(lane >= back, rolled, tail[k, rows, :])
            tail[k, rows, :] = rolled
        sig = sigmoid(c)
        value = c * sig
        slope_ref[rows, :] = (sig + value * (1.0 - sig)).astype(LOW)
        return value

    for i in range(2):
        bc_ref[i * n_state : (i + 1) * n_state, :] = conv(
            pl.ds(inner + i * n_state, n_state)
        ).astype(LOW)

    def group(first, rows, parts):
        xs = conv(rows)
        xs_ref[rows, :] = xs.astype(LOW)
        xd = jnp.concatenate([xs[own, :] * scale[h, :] for h, own in parts], axis=0).astype(LOW)
        fresh = contract(xd, bc_ref[:n_state, :], 1, 1)
        old = state[rows, :]
        sin_ref[0, rows, :] = old.astype(LOW)
        state[rows, :] = jnp.concatenate(
            [ewend[h, :] * old[own, :] + fresh[own, :] for h, own in parts], axis=0
        )

    grouped(heads, width, group)

    @pl.when(step == pl.num_programs(0) - 1)
    def _():
        send_ref[:inner, :] = state[...].astype(LOW)
        send_ref[inner:, :] = jnp.exp(offset[...]).astype(LOW)


def scan_states(u, chan, taps, bias, rate, heads, n_state):
    channels = chan.shape[0]
    length = u.shape[1] - BLOCK
    inner = channels - 2 * n_state
    blocks = length // BLOCK
    return call(
        states_kernel,
        (blocks,),
        [
            tokens(u, lambda b: b, channels),
            tokens(u, lambda b: blocks, channels),
            tokens(u, lambda b: b, heads, channels // heads),
            whole(chan), whole(bias), whole(rate),
        ],
        [
            token_out(inner, length, LOW),
            token_out(channels, length, LOW),
            token_out(2 * n_state, length, LOW),
            token_out(heads, length, F32),
            token_out(heads, length, F32),
            token_out(heads, length, F32),
            (out((length, heads), F32), pl.BlockSpec((BLOCK, heads), lambda b: (b, 0))),
            (
                out((blocks, inner, n_state), LOW),
                pl.BlockSpec((1, inner, n_state), lambda b: (b, 0, 0)),
            ),
            fixed_out((inner + heads, n_state), LOW),
        ],
        [
            pltpu.VMEM((taps - 1, channels, BLOCK), F32),
            pltpu.VMEM((inner, n_state), F32),
            pltpu.VMEM((heads, BLOCK), F32),
            pltpu.VMEM((heads, BLOCK), F32),
            pltpu.VMEM((heads, BLOCK), F32),
            pltpu.VMEM((taps, channels, BLOCK), F32),
            pltpu.VMEM((channels, BLOCK), F32),
        ],
        2 * length * inner * n_state,
        channels * length * 8,
        channels * length,
    )


def spread_columns(wcol_ref, wb):
    for h in range(wb.shape[0]):
        wb[h] = jnp.broadcast_to(wcol_ref[:, h : h + 1] * LOG2E, (BLOCK, BLOCK))


def masked_scores(bc_ref, n_state):
    scores = contract(bc_ref[:n_state, :], bc_ref[n_state:, :], 0, 0)
    return jnp.where(ordered(), scores, 0.0)


def decay(wrow, wb_h):
    return jnp.exp2(jnp.minimum(wrow * LOG2E - wb_h, 0.0))


def local_kernel(xs_ref, bc_ref, dt_ref, w_ref, wcol_ref, sin_ref, y_ref, wb, scores):
    heads = dt_ref.shape[0]
    inner = xs_ref.shape[0]
    width = inner // heads
    n_state = bc_ref.shape[0] // 2
    spread_columns(wcol_ref, wb)
    scores[...] = masked_scores(bc_ref, n_state)

    def group(first, rows, parts):
        entering = contract(sin_ref[0, rows, :], bc_ref[n_state:, :], 1, 0)
        xs = xs_ref[rows, :].astype(F32)
        result = []
        for i, (h, own) in enumerate(parts):
            wrow = w_ref[h, :]
            xdt = (xs[own, :] * dt_ref[h, :]).astype(LOW)
            weights = (scores[...] * decay(wrow, wb[first + i])).astype(LOW)
            result.append(entering[own, :] * jnp.exp(wrow) + contract(xdt, weights, 1, 0))
        y_ref[rows, :] = jnp.concatenate(result, axis=0).astype(y_ref.dtype)

    grouped(heads, width, group)


def scan_local(xs, bc, dt, w, wcol, sin):
    inner, length = xs.shape
    heads = dt.shape[0]
    return call(
        local_kernel,
        (length // BLOCK,),
        [
            tokens(xs),
            tokens(bc),
            tokens(dt),
            tokens(w),
            (wcol, pl.BlockSpec((BLOCK, heads), lambda b: (b, 0))),
            (sin, pl.BlockSpec((1,) + sin.shape[1:], lambda b: (b, 0, 0))),
        ],
        [token_out(inner, length, LOW)],
        [pltpu.VMEM((heads, BLOCK, BLOCK), F32), pltpu.VMEM((BLOCK, BLOCK), F32)],
        2 * length * inner * (BLOCK * 4 + bc.shape[0] // 2),
        inner * length * 6,
        heads * length * BLOCK,
    )[0]


def gate_kernel(
    yl_ref, xs_ref, z_ref, bc_ref, wt_ref, sdev_ref, skip_ref, gain_ref,
    ylow_ref, halves_ref, gated_ref, v_scr, total, *, order,
):
    inner = yl_ref.shape[0]
    heads = wt_ref.shape[0]
    width = inner // heads
    half = width // 2
    n_state = bc_ref.shape[0] // 2
    total[...] = jnp.zeros_like(total)

    def group(first, rows, parts):
        corr = contract(sdev_ref[rows, :], bc_ref[n_state:, :], 1, 0)
        xs = xs_ref[rows, :].astype(F32)
        extra = jnp.concatenate(
            [jnp.exp(wt_ref[h, :]) * corr[own, :] + skip_ref[h, :] * xs[own, :] for h, own in parts],
            axis=0,
        )
        y = (yl_ref[rows, :].astype(F32) + extra).astype(LOW)
        ylow_ref[rows, :] = y
        z = z_ref[rows, :].astype(F32)
        v = y.astype(F32) * (z * sigmoid(z))
        v_scr[rows, :] = v
        total[...] += fold(v * v)

    grouped(heads, width, group)
    r = lax.rsqrt(column_sum(total[...]) / inner + EPSILON)
    for h in range(heads):
        rows = slice(h * width, (h + 1) * width)
        gated = (v_scr[rows, :] * r * gain_ref[rows, :]).astype(LOW)
        for c in range(2):
            piece = gated[c * half : (c + 1) * half, :]
            halves_ref[c, h * half : (h + 1) * half, :] = piece
            if order is None:
                gated_ref[h * width + c * half : h * width + (c + 1) * half, :] = piece
            else:
                at = order[h][1] * half
                gated_ref[order[h][0], c, at : at + half, :] = piece


def gate_forward(yl, xs, z, bc, wt, sdev, skip, gain, order):
    inner, length = yl.shape
    heads = wt.shape[0]
    if order is None:
        gated = token_out(inner, length, LOW)
    else:
        shape = (2, 2, inner // 4)
        gated = (
            out(shape + (length,), LOW), pl.BlockSpec(shape + (BLOCK,), lambda b: (0, 0, 0, b))
        )
    pair = (2, inner // 2)
    halves = (out(pair + (length,), LOW), pl.BlockSpec(pair + (BLOCK,), lambda b: (0, 0, b)))
    return call(
        functools.partial(gate_kernel, order=order),
        (length // BLOCK,),
        [
            tokens(yl), tokens(xs), tokens(z), tokens(bc), tokens(wt), whole(sdev), whole(skip), whole(gain),
        ],
        [token_out(inner, length, LOW), halves, gated],
        [
            pltpu.VMEM((inner, BLOCK), F32),
            pltpu.VMEM((8, BLOCK), F32),
        ],
        2 * length * inner * sdev.shape[1],
        inner * length * 14,
        inner * length,
    )


def gate_back_kernel(
    dg0_ref, dg1_ref, ylow_ref, z_ref, bc_ref, wt_ref, gain_ref, decays_ref,
    dy_ref, dz_ref, gsum_ref, send_ref, ds, gg, sums, sig_scr, dg_ref,
):
    step = pl.program_id(0)
    inner = ylow_ref.shape[0]
    heads = wt_ref.shape[0]
    width = inner // heads
    n_state = bc_ref.shape[0] // 2

    @pl.when(step == 0)
    def _():
        gg[...] = jnp.zeros_like(gg)
        ds[...] = jnp.zeros_like(ds)

    sums[...] = jnp.zeros_like(sums)
    half = width // 2

    def first_pass(first, rows, parts):
        own = pl.ds(pl.multiple_of(first * half, len(parts) * half), len(parts) * half)
        both = [ref[own, :].astype(F32) for ref in (dg0_ref, dg1_ref)]
        dg_ref[rows, :] = jnp.concatenate(
            [both[c][i * half : (i + 1) * half, :] for i in range(len(parts)) for c in range(2)], axis=0
        )
        z = z_ref[rows, :].astype(F32)
        sig = sigmoid(z)
        sig_scr[rows, :] = sig
        v = ylow_ref[rows, :].astype(F32) * (z * sig)
        m = v * (dg_ref[rows, :] * gain_ref[rows, :])
        sums[0] += fold(v * v)
        sums[1] += fold(m)

    grouped(heads, width, first_pass)
    r = lax.rsqrt(column_sum(sums[0]) / inner + EPSILON)
    back = r * r * r * (column_sum(sums[1]) / inner)

    def second_pass(first, rows, parts):
        z = z_ref[rows, :].astype(F32)
        sig = sig_scr[rows, :]
        silu = z * sig
        y = ylow_ref[rows, :].astype(F32)
        v = y * silu
        du = dg_ref[rows, :]
        dv = r * (gain_ref[rows, :] * du) - v * back
        dy = (dv * silu).astype(LOW)
        dy_ref[rows, :] = dy
        dz_ref[rows, :] = (dv * y * (sig + silu * (1.0 - sig))).astype(LOW)
        gg[rows, :] += du * v * r
        dy = dy.astype(F32)
        dye = jnp.concatenate([dy[own, :] * jnp.exp(wt_ref[h, :]) for h, own in parts], axis=0)
        ds[rows, :] += contract(dye.astype(LOW), bc_ref[n_state:, :], 1, 1)

    grouped(heads, width, second_pass)

    @pl.when(step == pl.num_programs(0) - 1)
    def _():
        send_ref[:inner, :] = ds[...].astype(LOW)
        send_ref[inner:, :] = decays_ref[...]
        gsum_ref[:, 0:1] = jnp.sum(gg[...], axis=1, keepdims=True)


def gate_backward(dg0, dg1, ylow, z, bc, wt, gain, decays):
    inner, length = ylow.shape
    heads = wt.shape[0]
    n_state = bc.shape[0] // 2
    return call(
        gate_back_kernel,
        (length // BLOCK,),
        [
            tokens(dg0), tokens(dg1),
            tokens(ylow), tokens(z), tokens(bc), tokens(wt), whole(gain), whole(decays),
        ],
        [
            token_out(inner, length, LOW),
            token_out(inner, length, LOW),
            fixed_out((inner, 8), F32),
            fixed_out((inner + heads, n_state), LOW),
        ],
        [
            pltpu.VMEM((inner, n_state), F32),
            pltpu.VMEM((inner, BLOCK), F32),
            pltpu.VMEM((2, 8, BLOCK), F32),
            pltpu.VMEM((inner, BLOCK), F32),
            pltpu.VMEM((inner, BLOCK), F32),
        ],
        0,
        0,
    )


def local_back_kernel(
    xs_ref, dy_ref, bc_ref, dt_ref, w_ref, wcol_ref, dx_ref, rows_ref, dbc_ref, wb, scores, dscores
):
    heads = dt_ref.shape[0]
    inner = xs_ref.shape[0]
    width = inner // heads
    n_state = bc_ref.shape[0] // 2
    spread_columns(wcol_ref, wb)
    scores[...] = masked_scores(bc_ref, n_state)
    dscores[...] = jnp.zeros_like(dscores)

    def group(first, rows, parts):
        xs = xs_ref[rows, :].astype(F32)
        dy_all = dy_ref[rows, :]
        result, total = [], 0.0
        for i, (h, own) in enumerate(parts):
            xdt = (xs[own, :] * dt_ref[h, :]).astype(LOW)
            dy = dy_all[own, :]
            decays = decay(w_ref[h, :], wb[first + i])
            weights = (scores[...] * decays).astype(LOW)
            y = contract(xdt, weights, 1, 0)
            dx = contract(dy, weights, 1, 1)
            total = total + decays * contract(xdt, dy, 0, 0)
            result.append(dx)
            rows_ref[h, :] = column_sum(dy.astype(F32) * y - xdt.astype(F32) * dx)
        dscores[...] += total
        dx_ref[rows, :] = jnp.concatenate(result, axis=0).astype(dx_ref.dtype)

    grouped(heads, width, group)
    masked = jnp.where(ordered(), dscores[...], 0.0).astype(LOW)
    dbc_ref[:n_state, :] = contract(bc_ref[n_state:, :], masked, 1, 1)
    dbc_ref[n_state:, :] = contract(bc_ref[:n_state, :], masked, 1, 0)


def scan_local_back(xs, dy, bc, dt, w, wcol):
    inner, length = xs.shape
    heads = dt.shape[0]
    return call(
        local_back_kernel,
        (length // BLOCK,),
        [
            tokens(xs),
            tokens(dy),
            tokens(bc),
            tokens(dt),
            tokens(w),
            (wcol, pl.BlockSpec((BLOCK, heads), lambda b: (b, 0))),
        ],
        [
            token_out(inner, length, LOW),
            token_out(heads, length, F32),
            token_out(bc.shape[0], length, F32),
        ],
        [
            pltpu.VMEM((heads, BLOCK, BLOCK), F32),
            pltpu.VMEM((BLOCK, BLOCK), F32),
            pltpu.VMEM((BLOCK, BLOCK), F32),
        ],
        2 * length * inner * BLOCK * 12,
        inner * length * 6,
        heads * length * BLOCK,
    )


def states_back_kernel(
    u_ref, halo_ref, step_ref, slope_ref, xs_ref, dy_ref, dxl_ref, dbcl_ref, bc_ref,
    dt_ref, w_ref, wt_ref, rows_ref, sin_ref, sdev_ref, dsend_ref,
    chan_ref, bias_ref, rate_ref, skip_ref,
    du_ref, first_ref, csum_ref, hsum_ref,
    ds, toend, ew, ewend, offs, rr, kk, ddt, ee, right, gconv, ghead, dbc, dc_first, cw_ref,
):
    step = pl.program_id(0)
    final = pl.num_programs(0) - 1
    heads = step_ref.shape[0]
    inner = xs_ref.shape[0]
    channels = u_ref.shape[0]
    width = inner // heads
    n_state = bc_ref.shape[0] // 2
    taps = cw_ref.shape[0]
    subs = sin_ref.shape[0]
    spans = [slice(s * BLOCK, (s + 1) * BLOCK) for s in range(subs)]
    backwards = list(reversed(range(subs)))

    @pl.when(step == 0)
    def _():
        ds[...] = dsend_ref[...]
        for k in range(taps):
            spread_lanes(chan_ref, k, cw_ref.at[k])
        right[...] = jnp.zeros_like(right)
        gconv[...] = jnp.zeros_like(gconv)
        ghead[...] = jnp.zeros_like(ghead)

    for s in range(subs):
        w = w_ref[:, spans[s]]
        wend = jnp.broadcast_to(w[:, BLOCK - 1 :], w.shape)
        toend[s] = jnp.exp(wend - w)
        ew[s] = jnp.exp(w)
        ewend[s] = jnp.exp(wend)
        offs[s] = jnp.exp(wt_ref[:, spans[s]] - w)
        dbc[s] = dbcl_ref[:, spans[s]]

    def conv_back(rows, dxs):
        lane = lax.broadcasted_iota(jnp.int32, (1, BLOCK), 1)
        carried = [right[k, rows, :] for k in range(taps - 1)]
        sums = [gconv[k, rows, :] for k in range(taps + 1)]
        for s in backwards:
            u = u_ref[rows, spans[s]].astype(F32)
            dc = dxs[s] * slope_ref[rows, spans[s]].astype(F32)
            du = cw_ref[taps - 1, rows, :] * dc
            sums[taps - 1] = sums[taps - 1] + u * dc
            sums[taps] = sums[taps] + dc
            for k in range(taps - 1):
                ahead = taps - 1 - k
                rolled = pltpu.roll(dc, BLOCK - ahead, 1)
                moved = jnp.where(lane < BLOCK - ahead, rolled, carried[k])
                carried[k] = rolled
                du = du + cw_ref[k, rows, :] * moved
                sums[k] = sums[k] + u * moved
            du_ref[rows, spans[s]] = du.astype(LOW)
        for k in range(taps - 1):
            right[k, rows, :] = carried[k]
        for k in range(taps + 1):
            gconv[k, rows, :] = sums[k]
        dc_first[rows, :] = dc

    def group(first, rows, parts):
        sdev = sdev_ref[rows, :].astype(F32)
        d = ds[rows, :]
        b_low = bc_ref[:n_state, :]
        c_low = bc_ref[n_state:, :]
        all_dxs = [None] * subs
        for s in backwards:
            sin = sin_ref[s, rows, :].astype(F32)
            entering = jnp.concatenate(
                [sin[own, :] + offs[s, h, :] * sdev[own, :] for h, own in parts], axis=0
            )
            cross = d * entering
            for h, own in parts:
                ee[s, h, :] = ewend[s, h, :] * column_sum(cross[own, :])
            d_low = d.astype(LOW)
            entering_low = entering.astype(LOW)
            q = contract(d_low, b_low[:, spans[s]], 1, 0)
            yo = contract(entering_low, c_low[:, spans[s]], 1, 0)
            xs = xs_ref[rows, spans[s]].astype(F32)
            dy = dy_ref[rows, spans[s]].astype(F32)
            dxl = dxl_ref[rows, spans[s]].astype(F32)
            xde, dye, dxs = [], [], []
            for h, own in parts:
                te, eh, dt = toend[s, h, :], ew[s, h, :], dt_ref[h, spans[s]]
                x, g = xs[own, :], dy[own, :]
                xe = x * dt * te
                ge = g * eh
                kk[s, h, :] = column_sum(xe * q[own, :])
                rr[s, h, :] = rows_ref[h, spans[s]] + column_sum(ge * yo[own, :])
                xde.append(xe)
                dye.append(ge)
                dx = dxl[own, :] + te * q[own, :]
                ddt[s, h, :] = column_sum(dx * x)
                ghead[2, h, :] += column_sum(g * x)
                dxs.append(dx * dt + skip_ref[h, :] * g)
            xde = jnp.concatenate(xde, axis=0).astype(LOW)
            dye = jnp.concatenate(dye, axis=0).astype(LOW)
            dbc[s, :n_state, :] += contract(d_low, xde, 0, 0)
            dbc[s, n_state:, :] += contract(entering_low, dye, 0, 0)
            fresh = contract(dye, c_low[:, spans[s]], 1, 1)
            d = jnp.concatenate(
                [ewend[s, h, :] * d[own, :] + fresh[own, :] for h, own in parts], axis=0
            )
            all_dxs[s] = jnp.concatenate(dxs, axis=0)
        ds[rows, :] = d
        conv_back(rows, all_dxs)

    grouped(heads, width, group)
    for i in range(2):
        at = slice(i * n_state, (i + 1) * n_state)
        conv_back(pl.ds(inner + i * n_state, n_state), [dbc[s, at, :] for s in range(subs)])

    upper = ordered().astype(F32)
    rate = rate_ref[...]
    for s in range(subs):
        dloga = (
            contract(rr[s], upper, 1, 1, HIGHEST)
            + (contract(kk[s], upper, 1, 0, HIGHEST) - kk[s])
            + jnp.sum(ee[s], axis=1, keepdims=True)
        )
        dt = dt_ref[:, spans[s]]
        raw = step_ref[:, spans[s]].astype(F32) + bias_ref[...]
        dstep = (ddt[s] + dloga * rate) * sigmoid(raw)
        du_ref[channels:, spans[s]] = dstep.astype(LOW)
        ghead[0] += dstep
        ghead[1] += dloga * dt * rate

    @pl.when(step == final)
    def _():
        first_ref[...] = dc_first[...].T[: first_ref.shape[0], :]
        lane = lax.broadcasted_iota(jnp.int32, (1, BLOCK), 1)
        size = channels // 8

        def sums(i, carry):
            rows = pl.ds(pl.multiple_of(i * size, 16), size)
            halo = halo_ref[rows, :].astype(F32)
            dc = dc_first[rows, :]
            for k in range(taps + 1):
                total = gconv[k, rows, :]
                if k < taps - 1:
                    back = taps - 1 - k
                    total = total + jnp.where(lane < back, pltpu.roll(halo, back, 1) * dc, 0.0)
                csum_ref[rows, k : k + 1] = jnp.sum(total, axis=1, keepdims=True)
            return carry

        lax.fori_loop(0, 8, sums, 0)
        for i in range(3):
            hsum_ref[:, i : i + 1] = jnp.sum(ghead[i], axis=1, keepdims=True)


def scan_states_back(
    u, slope, xs, dy, dx_local, dbc_local, bc, dt, w, wt, row_sums, sin, sdev, dsend,
    chan, taps, bias, rate, skip,
):
    channels, length = slope.shape
    heads = dt.shape[0]
    inner = xs.shape[0]
    steps = length // (SUBS * BLOCK)
    n_state = bc.shape[0] // 2
    span = SUBS * BLOCK
    place = lambda b: steps - 1 - b

    def pairs(array, rows=None, at=0):
        rows = array.shape[0] if rows is None else rows
        return (array, pl.BlockSpec((rows, span), lambda b: (at, place(b))))

    def pairs_out(rows, dtype):
        return (out((rows, length), dtype), pl.BlockSpec((rows, span), lambda b: (0, place(b))))

    per_head = pltpu.VMEM((SUBS, heads, BLOCK), F32)
    return call(
        states_back_kernel,
        (steps,),
        [
            pairs(u, channels),
            tokens(u, lambda b: length // BLOCK, channels),
            pairs(u, heads, channels // heads),
            pairs(slope),
            pairs(xs),
            pairs(dy),
            pairs(dx_local),
            pairs(dbc_local),
            pairs(bc),
            pairs(dt),
            pairs(w),
            pairs(wt),
            pairs(row_sums),
            (sin, pl.BlockSpec((SUBS,) + sin.shape[1:], lambda b: (place(b), 0, 0))),
            whole(sdev),
            whole(dsend),
            whole(chan),
            whole(bias),
            whole(rate),
            whole(skip),
        ],
        [
            pairs_out(channels + heads, LOW),
            fixed_out((8, channels), F32),
            fixed_out((channels, 8), F32),
            fixed_out((heads, 8), F32),
        ],
        [
            pltpu.VMEM((inner, n_state), F32),
            per_head,
            per_head,
            per_head,
            per_head,
            per_head,
            per_head,
            per_head,
            per_head,
            pltpu.VMEM((taps - 1, channels, BLOCK), F32),
            pltpu.VMEM((taps + 1, channels, BLOCK), F32),
            pltpu.VMEM((3, heads, BLOCK), F32),
            pltpu.VMEM((SUBS, 2 * n_state, BLOCK), F32),
            pltpu.VMEM((channels, BLOCK), F32),
            pltpu.VMEM((taps, channels, BLOCK), F32),
        ],
        2 * length * inner * n_state * 5,
        inner * length * 14 + taps * channels * 1024,
        channels * length,
    )


def edge_kernel(du_ref, ahead_ref, chan_ref, out_ref, *, taps):
    lanes = du_ref.shape[1]
    channels = ahead_ref.shape[1]
    lane = lax.broadcasted_iota(jnp.int32, (1, lanes), 1)
    for at in range(0, channels, lanes):
        rows = slice(at, at + lanes)
        ahead = jnp.concatenate(
            [ahead_ref[:, rows], jnp.zeros((lanes - ahead_ref.shape[0], lanes), F32)], axis=0
        ).T
        du = du_ref[rows, :].astype(F32)
        for k in range(taps - 1):
            back = taps - 1 - k
            moved = pltpu.roll(ahead, lanes - back, 1)
            du = du + jnp.where(lane >= lanes - back, chan_ref[rows, k : k + 1] * moved, 0.0)
        out_ref[rows, :] = du.astype(LOW)


def add_edge(du, ahead, chan, taps):
    channels = ahead.shape[1]
    last = du.shape[1] // BLOCK - 1
    block = pl.BlockSpec((channels, BLOCK), lambda b: (0, last))
    return pl.pallas_call(
        functools.partial(edge_kernel, taps=taps),
        grid=(1,),
        in_specs=[block, whole(ahead)[1], whole(chan)[1]],
        out_specs=block,
        out_shape=out(du.shape, LOW),
        input_output_aliases={0: 0},
        compiler_params=pltpu.CompilerParams(vmem_limit_bytes=VMEM_BYTES),
        cost_estimate=pl.CostEstimate(flops=0, bytes_accessed=channels * 3000, transcendentals=0),
    )(du, ahead, chan)


def shifted(x, axis, by):
    devices = lax.axis_size(axis)
    return lax.ppermute(
        x, axis, [(i, i + by) for i in range(devices) if 0 <= i + by < devices]
    )


def swapped(x):
    return lax.ppermute(x, "section", [(0, 1), (1, 0)])


def after(value, *others):
    return lax.optimization_barrier((value,) + others)[0]


def summed(value, axes):
    for axis in axes:
        reach = 1
        while reach < lax.axis_size(axis):
            pairs = [(i, i ^ reach) for i in range(lax.axis_size(axis))]
            value = value + lax.ppermute(value, axis, pairs)
            reach *= 2
    return value


def chained(own, inner, heads, toward, beside):
    devices = lax.axis_size("head")
    shape = (heads, inner // heads, own.shape[1])
    split = lambda a: (a[:inner].astype(F32).reshape(shape), a[inner:].astype(F32)[:, :1, None])
    if devices <= 4:
        got = [shifted(own, "head", toward * k) for k in range(1, devices)]
        terms = [split(a) for a in lax.optimization_barrier((*got, beside))[:-1]]
        total = terms[-1][0]
        for state, factor in terms[-2::-1]:
            total = state + factor * total
        return total.reshape(inner, own.shape[1])
    index = lax.axis_index("head")
    everyone = lax.all_gather(own, "head", axis=0)
    total = jnp.zeros(shape, F32)
    for m in range(devices) if toward == 1 else range(devices - 1, -1, -1):
        state, factor = split(everyone[m])
        before = (m < index) if toward == 1 else (m > index)
        total = jnp.where(before, total * factor + state, total)
    return total.reshape(inner, own.shape[1])


def gathered(in_shard, out_shard, joined):
    section = lax.axis_index("section")
    layers = lax.axis_size("section")
    rows = in_shard.shape[0]
    model = out_shard.shape[1]
    across = ("seq", "head", "section")
    halves = lambda a: a.reshape((2, a.shape[0] // 2) + a.shape[1:])

    def pieces(a):
        a = halves(a)
        own = lax.dynamic_index_in_dim(a, section, 0, keepdims=False)
        got = swapped(lax.dynamic_index_in_dim(a, 1 - section, 0, keepdims=False))
        return [jnp.where(section == i, own, got) for i in range(layers)]

    everyone = lambda a: lax.all_gather(a, across, axis=0, tiled=True)
    result = []
    if joined:
        side = out_shard.reshape(2, 2, rows // 2, model).transpose(0, 2, 1, 3).reshape(rows, 2 * model)
        first, *others = pieces(jnp.concatenate([side, in_shard], axis=1))
        every = everyone(first)
        result.append((lambda since: every[:, : 2 * model], every[:, 2 * model :]))
        for piece in others:
            w_in = everyone(piece[:, 2 * model :])
            result.append(
                (lambda since, piece=piece: everyone(after(piece[:, : 2 * model], since)), w_in)
            )
        return result
    for in_piece, out_piece in zip(pieces(in_shard), pieces(out_shard)):
        w_in = everyone(in_piece)
        result.append((lambda since, out_piece=out_piece: everyone(out_piece), w_in))
    return result


def products(left, rights, index):
    return jnp.concatenate(
        [
            contract(lax.dynamic_index_in_dim(a, index, 0, keepdims=False), b, 1, dim)
            for a, (b, dim) in zip(left, rights)
        ],
        axis=1,
    )


def pair_sent(left, rights):
    return products(left, rights, 1 - lax.axis_index("section")).astype(LOW)


def pair_sum(left, rights, sent):
    own = products(left, rights, lax.axis_index("section"))
    return (own + swapped(sent).astype(F32)).astype(LOW)


def over_head(part, beside=()):
    count = lax.axis_size("head")
    rows, columns = part.shape
    part = after(lax.all_to_all(part, "head", split_axis=0, concat_axis=0, tiled=True), *beside)
    return jnp.sum(part.reshape(count, rows // count, columns).astype(F32), axis=0).astype(LOW)


def over_seq(part, beside=()):
    count = lax.axis_size("seq")
    rows, columns = part.shape
    part = after(lax.all_to_all(part, "seq", split_axis=0, concat_axis=0, tiled=True), *beside)
    return jnp.sum(part.reshape(count, rows // count, columns).astype(F32), axis=0)


def over_both(part):
    return lax.psum_scatter(part, ("head", "seq"), scatter_dimension=0, tiled=True).astype(F32)


def by_owner(values, split):
    seqs, heads_n = lax.axis_size("seq"), lax.axis_size("head")
    rows, columns = values.shape
    own = rows // (seqs * heads_n * 2 * split)
    values = values.reshape(seqs, heads_n, 2, split, own, columns)
    return values.transpose(2, 3, 1, 0, 4, 5).reshape(2, split, seqs * heads_n * own, columns)


def rms_inverse(h):
    return lax.rsqrt(jnp.mean(h * h, axis=-1, keepdims=True) + EPSILON)


def spread(values):
    return jnp.broadcast_to(values[..., None], values.shape + (BLOCK,))


def columns(*vectors):
    rows = [v[None] for v in vectors]
    rows.append(jnp.zeros((8 - len(vectors), vectors[0].shape[0]), F32))
    return jnp.concatenate(rows, axis=0).T


def first_norm(h, p):
    normed = (h * rms_inverse(h) * p["norm_gain"]).astype(LOW)
    edge = shifted(after(h[-8:], *p["early"]), "head", 1)
    edge = (edge * rms_inverse(edge) * p["norm_gain"]).astype(LOW)
    padded = jnp.concatenate([normed, jnp.zeros((BLOCK - 8, h.shape[1]), LOW), edge], axis=0)
    return normed, padded


def layer_forward(h, normed, padded, p):
    inner, n_state, heads = p["inner"], p["n_state"], p["heads"]
    u = contract(p["w_x"], padded, 0, 1).astype(LOW)
    z = contract(p["w_z"], normed, 0, 1).astype(LOW)
    xs, slope, bc, dt, w, wt, wcol, sin, send = scan_states(
        u, p["chan"], p["taps"], p["bias"], p["rate"], heads, n_state
    )
    y_local = scan_local(xs, bc, dt, w, wcol, sin)
    sdev = chained(send, inner, heads, 1, y_local).astype(LOW)
    ylow, halves, gated = gate_forward(
        y_local, xs, z, bc, wt, sdev, p["skip"], p["gate_gain"], p["order"]
    )
    if p["order"] is None:
        gated = by_owner(gated, 2)
    result = h + contract(halves[0], p["w_o"][0], 0, 0) + contract(halves[1], p["w_o"][1], 0, 0)
    kept = dict(
        h=h, normed_rows=by_owner(normed.T, 1)[:, 0], z=z, u=u, slope=slope, xs=xs, bc=bc, dt=dt, w=w, wt=wt,
        wcol=wcol, sin=sin, sdev=sdev, ylow=ylow, gated=gated, decays=send[inner:],
    )
    return result, kept


def layer_backward(g, p, k, finished, pending):
    inner, n_state, heads, last, taps = p["inner"], p["n_state"], p["heads"], p["last"], p["taps"]
    g_low = after(g.astype(LOW), *finished)
    dg = [contract(w, g_low, 1, 1).astype(LOW) for w in p["w_o"]]
    if last:
        pending = over_head(pending)
    normed_rows = k["normed_rows"]
    dy, dz, gsum, send = gate_backward(
        dg[0], dg[1], k["ylow"], k["z"], k["bc"], k["wt"], p["gate_gain"], k["decays"]
    )
    left = [k["gated"][:, 0], k["gated"][:, 1], normed_rows]
    rights = [(g_low, 0), (g_low, 0), (dz, 1)]
    sent = pair_sent(left, rights)
    if last:
        sent = after(sent, pending)
    dx_local, row_sums, dbc_local = scan_local_back(
        k["xs"], after(dy, sent), k["bc"], k["dt"], k["w"], k["wcol"]
    )
    if last:
        pending = over_seq(pending, (dx_local,))
    dsend = chained(send, inner, heads, -1, dx_local)
    early = pair_sum(left, rights, sent)
    du, first, csum, hsum = scan_states_back(
        k["u"], k["slope"], k["xs"], dy, after(dx_local, early), dbc_local, k["bc"], k["dt"], k["w"],
        k["wt"], row_sums, k["sin"], k["sdev"], dsend, p["chan"], p["taps"], p["bias"], p["rate"], p["skip"],
    )
    ahead = shifted(first, "head", -1)
    dnormed = contract(after(dz, first), p["w_z"], 0, 1)
    if last:
        early = over_head(after(early, dsend, dx_local, pending), (dnormed,))
        du = after(du, early, dnormed)
        early = over_seq(early)
    else:
        early = over_both(early)
        du = after(du, dnormed)
    du = add_edge(du, ahead, p["chan"], taps)
    left, rights = [normed_rows], [(du, 1)]
    sent = pair_sent(left, rights)
    late = pair_sum(left, rights, after(sent, early) if last else sent)
    dnormed = dnormed + contract(after(du, late), p["w_x"], 0, 1)
    h = k["h"]
    r = rms_inverse(h)
    wd = dnormed * p["norm_gain"]
    dh = r * wd - h * (r * r * r * jnp.mean(wd * h, axis=-1, keepdims=True))
    small = jnp.concatenate(
        [
            jnp.sum(dnormed * h * r, axis=0),
            csum[:, : taps + 1].T.reshape(-1),
            hsum[:, :3].T.reshape(-1),
            gsum[:, 0],
        ]
    )
    return g + dh, early, late, pending, small


def local(
    section_ends, norm_gain, in_weight, conv_weight, conv_bias, dt_bias, a_log, skip_gain, gated_gain, out_weight,
):
    section = lax.axis_index("section")
    layers = lax.axis_size("section")
    seqs, heads_n = lax.axis_size("seq"), lax.axis_size("head")
    inner = gated_gain.shape[1]
    heads = dt_bias.shape[1]
    width = inner // heads
    n_state = (conv_bias.shape[1] - inner) // 2
    model = norm_gain.shape[1]
    ends = section_ends[0, :, 0]
    turned = jnp.where(section == 0, ends[1], ends[0])
    received = swapped(turned)
    hidden = jnp.where(section == 0, ends[0], received)
    cotangent = jnp.where(section == 0, received, ends[1])

    joined = out_weight.shape[1] == 2 * width and in_weight.shape[1] == width
    weights = gathered(in_weight[0].astype(LOW), out_weight[0].astype(LOW), joined)
    mine = (norm_gain, conv_weight, conv_bias, dt_bias, a_log, skip_gain, gated_gain)
    flat = jnp.concatenate([a.reshape(-1) for a in mine])
    other = swapped(flat)
    params = []
    for i in range(layers):
        own = jnp.where(section == i, flat, other)
        parts, at = [], 0
        for a in mine:
            parts.append(own[at : at + a.size].reshape(a.shape[1:]))
            at += a.size
        gain, cw, cb, bias, alog, skip, gate_gain = parts
        w_out, w_in = weights[i]
        order = tuple((h % 2, (h // 2 % heads_n) * seqs + h // 2 // heads_n) for h in range(heads))
        params.append(
            dict(
                inner=inner,
                n_state=n_state,
                heads=heads,
                order=order if joined else None,
                last=i == 0,
                norm_gain=gain,
                w_z=w_in[:, :inner],
                w_x=w_in[:, inner:],
                w_out=w_out,
                taps=cw.shape[0],
                chan=columns(*cw, cb),
                bias=spread(bias),
                rate=spread(-jnp.exp(alog)),
                skip=spread(skip),
                gate_gain=spread(gate_gain),
            )
        )

    prepared = [p[name] for p in params for name in ("chan", "bias", "rate", "skip", "gate_gain")]
    params[0]["early"] = prepared
    params[1]["early"] = []
    kept = []
    for p in params:
        normed, padded = first_norm(hidden, p)
        if kept:
            padded = after(padded, kept[-1]["normed_rows"])
        w_out = p["w_out"](kept[-1]["u"] if kept else None)
        if joined:
            p["w_o"] = (w_out[:, :model], w_out[:, model:])
        else:
            w_o = w_out.reshape(heads, 2, width // 2, model).transpose(1, 0, 2, 3)
            p["w_o"] = w_o.reshape(2, inner // 2, model)
        hidden, k = layer_forward(hidden, normed, padded, p)
        kept.append(k)
    hidden_other = lax.ppermute(hidden, "section", [(0, 1)])
    grad = after(cotangent, hidden)
    grad, early_1, late_1, _, small_1 = layer_backward(grad, params[1], kept[1], [], None)
    grad, early_0, late_0, late_1, small_0 = layer_backward(
        grad, params[0], kept[0], [early_1], late_1
    )
    grad_other = lax.ppermute(grad, "section", [(1, 0)])
    first = section == 0
    ends_out = jnp.stack(
        [jnp.where(first, grad, hidden_other), jnp.where(first, grad_other, hidden)]
    )

    total = jnp.where(first, small_0, small_1) + swapped(jnp.where(first, small_1, small_0))
    total = summed(total, ("head", "seq"))
    grads, at = [], 0
    for a in (norm_gain, conv_weight, conv_bias, dt_bias, a_log, skip_gain, gated_gain):
        grads.append(total[at : at + a.size].reshape(a.shape))
        at += a.size
    norm_g, conv_g, shift_g, bias_g, alog_g, skip_g, gate_g = grads
    late_0 = over_seq(over_head(late_0))
    rows = [
        jnp.concatenate([early_0, after(late_0, *grads)], axis=1),
        jnp.concatenate([early_1, late_1], axis=1),
    ]
    got = swapped(jnp.where(first, rows[1], rows[0]))
    own = jnp.where(first, rows[0], rows[1])
    both = jnp.stack([jnp.where(first, own, got), jnp.where(first, got, own)])
    share = both.shape[1]
    out_rows = both[:, :, : 2 * model].reshape(2, share, 2, model).transpose(0, 2, 1, 3)
    out_rows = out_rows.reshape(4 * share, model)
    in_rows = both[:, :, 2 * model :].reshape(2 * share, -1)

    return (
        ends_out[None, :, None], norm_g, in_rows[None], conv_g, shift_g, bias_g, alog_g, skip_g, gate_g,
        out_rows[None],
    )


def solution(mesh):
    in_specs = (
        P("section", None, "seq", "head", None),
        P("section", None),
        P("section", ("seq", "head"), None),
        P("section", None, None),
        P("section", None),
        P("section", None),
        P("section", None),
        P("section", None),
        P("section", None),
        P("section", ("seq", "head"), None),
    )
    return jax.shard_map(local, mesh=mesh, in_specs=in_specs, out_specs=in_specs, check_vma=False)
```

profile of v0, /device:TPU:0, one launch (start us, length us, event | category | flops | bytes accessed | tf_op | source)
XLA Modules:
  0.0 778.9 jit_solution(12587284519693791427)
XLA Ops:
  13.5 6.9 bitcast_select_fusion.1
  21.1 6.4 collective-permute-done.2
  31.6 7.4 multiply_reduce_fusion.5
  46.3 4.8 collective-permute-start.3
  59.2 56.3 %all-gather.4.cloned.1.call-done = bf16[1024,6432]{1,0:T(8,128)(2,1)} async-done(((bf16[32,6432]{1,0:T(8,128)(2,1)}), bf16[1024,6432]{1,0:T(8,128)(2,1)}) %all-gather.4.cloned.1.call-update) | async-done | bytes 13172752 | tf_op jit(solution)/shard_map/all_gather | solution.py:822
  115.6 12.4 %convolution_convert_fusion.1.u_ref.halo_ref.step_ref = bf16[2336,1152]{1,0:T(8,128)(2,1)} fusion(bf16[1024,6432]{1,0:T(8,128)(2,1)} %all-gather.4.cloned.1.call-done, bf16[8,1024]{1,0:T(8,128)(2,1)S(1)} %multiply_convert_fusion.3, bf16[1024,1024]{1,0:T(8,128)(2,1)} %multiply_convert_fusion.1, bf16[1152]{0:T(1024)(128)(2,1)S(1)} %pad.24.clone), kind=kOutput, calls=%fused_computation.1 | convolution fusion | flops 5521084416 | bytes 12478720 | tf_op jit(solution)/shard_map/dot_general | solution.py:22
  128.0 17.1 %shard_map.177 = (bf16[2048,1024]{1,0:T(8,128)(2,1)}, bf16[2304,1024]{1,0:T(8,128)(2,1)}, bf16[256,1024]{1,0:T(8,128)(2,1)}, f32[32,1024]{1,0:T(8,128)}, f32[32,...) custom-call(bf16[2336,1152]{1,0:T(8,128)(2,1)} %convolution_convert_, ...), custom_call_target="tpu_custom_call" | custom-call | flops 536870912 | bytes 18874368 | tf_op jit(solution)/shard_map/pallas_call | solution.py:68
  145.1 4.2 collective-permute-start.6
  152.9 8.5 %convolution_convert_fusion.5.z_ref = bf16[2048,1024]{1,0:T(8,128)(2,1)} fusion(bf16[1024,1024]{1,0:T(8,128)(2,1)S(1)} %copy-done.18, bf16[1024,6432]{1,0:T(8,128)(2,1)} %all-gather.4.cloned.1.call-done), kind=kOutput, calls=%fused_computation.39 | convolution fusion | flops 4297064448 | bytes 10485760 | tf_op jit(solution)/shard_map/dot_general | solution.py:22
  161.4 11.8 %shard_map.178.yl_ref = bf16[2048,1024]{1,0:T(8,128)(2,1)} custom-call(bf16[2048,1024]{1,0:T(8,128)(2,1)} %get-tuple-element.90.xs_ref, bf16[256,1024]{1,0:T(8,128)(2,1)} %get-tuple-element.91.bc_ref, f32[32,1024]{1,0:T(8,128)} %get-tuple-element.92.dt_ref, f32[32,1024]{1,0:T(8,128)} %get-tuple-element.93.w_ref, f32[1024,32]{1,0:T(8,128)} %get-tuple-element.94.wcol_ref, ...), custom_call_target="tpu_custom_call" | custom-call | flops 2684354560 | bytes 12582912 | tf_op jit(solution)/shard_map/pallas_call | solution.py:68
  173.2 7.1 collective-permute-done.5
  183.2 14.6 %shard_map.179 = (bf16[2048,1024]{1,0:T(8,128)(2,1)}, bf16[2,1024,1024]{2,1,0:T(8,128)(2,1)}, bf16[2,2,512,1024]{3,2,1,0:T(8,128)(2,1)}) custom-call(bf16[2048,1024]{1,0:T(8,128)(2,1)} %shard_map.178.yl_ref, bf16[2048,1024]{1,0:T(8,128)(2,1)} %get-tuple-element.90.xs_ref, bf16[2048,1024]{1,0:T(8,128)(2,1)} %convolution_convert_fusion.5.z_ref, ...), custom_call_target="tpu_custom_call" | custom-call | flops 536870912 | bytes 29360128 | tf_op jit(solution)/shard_map/pallas_call | solution.py:68
  197.9 5.0 fusion.26
  202.9 4.6 multiply_reduce_fusion.4
  207.5 4.7 collective-permute-start.7
  212.7 8.6 %convolution_convert_fusion.4.z_ref = bf16[2048,1024]{1,0:T(8,128)(2,1)} fusion(bf16[1024,1024]{1,0:T(8,128)(2,1)S(1)} %multiply_convert_fusion, bf16[1024,4384]{1,0:T(8,128)(2,1)} %all-gather.6.cloned.1.call-done), kind=kOutput, calls=%fused_computation.38 | convolution fusion | flops 4297064448 | bytes 10485760 | tf_op jit(solution)/shard_map/dot_general | solution.py:22
  221.9 8.7 %convolution_convert_fusion.u_ref.halo_ref.step_ref = bf16[2336,1152]{1,0:T(8,128)(2,1)} fusion(bf16[1152,1024]{1,0:T(8,128)(2,1)S(1)} %pad_maximum_fusion.2, bf16[1024,4384]{1,0:T(8,128)(2,1)S(1)} %copy-done.49), kind=kOutput, calls=%fused_computation | convolution fusion | flops 5514006528 | bytes 12722176 | tf_op jit(solution)/shard_map/dot_general | solution.py:22
  230.7 17.2 %shard_map.180 = (bf16[2048,1024]{1,0:T(8,128)(2,1)}, bf16[2304,1024]{1,0:T(8,128)(2,1)}, bf16[256,1024]{1,0:T(8,128)(2,1)}, f32[32,1024]{1,0:T(8,128)}, f32[32,...) custom-call(bf16[2336,1152]{1,0:T(8,128)(2,1)} %convolution_convert_, ...), custom_call_target="tpu_custom_call" | custom-call | flops 536870912 | bytes 18874368 | tf_op jit(solution)/shard_map/pallas_call | solution.py:68
  261.3 11.6 %shard_map.181.yl_ref = bf16[2048,1024]{1,0:T(8,128)(2,1)} custom-call(bf16[2048,1024]{1,0:T(8,128)(2,1)} %get-tuple-element.103.xs_ref, bf16[256,1024]{1,0:T(8,128)(2,1)} %get-tuple-element.104.bc_ref, f32[32,1024]{1,0:T(8,128)} %get-tuple-element.105.dt_ref, f32[32,1024]{1,0:T(8,128)} %get-tuple-element.106.w_ref, f32[1024,32]{1,0:T(8,128)} %get-tuple-element.107.wcol_ref, ...), custom_call_target="tpu_custom_call" | custom-call | flops 2684354560 | bytes 12582912 | tf_op jit(solution)/shard_map/pallas_call | solution.py:68
  272.9 7.7 collective-permute-done.9
  283.5 14.8 %shard_map.182 = (bf16[2048,1024]{1,0:T(8,128)(2,1)}, bf16[2,1024,1024]{2,1,0:T(8,128)(2,1)}, bf16[2,2,512,1024]{3,2,1,0:T(8,128)(2,1)}) custom-call(bf16[2048,1024]{1,0:T(8,128)(2,1)} %shard_map.181.yl_ref, bf16[2048,1024]{1,0:T(8,128)(2,1)} %get-tuple-element.103.xs_ref, bf16[2048,1024]{1,0:T(8,128)(2,1)} %convolution_convert_fusion.4.z_ref, ...), custom_call_target="tpu_custom_call" | custom-call | flops 536870912 | bytes 29360128 | tf_op jit(solution)/shard_map/pallas_call | solution.py:68
  298.3 4.2 fusion.123
  302.5 5.4 fusion.20
  309.2 4.6 add_add_fusion
  318.9 3.7 convolution_convert_fusion.10.dg1_ref
  322.6 3.7 convolution_convert_fusion.11.dg0_ref
  326.3 17.3 %shard_map.183 = (bf16[2048,1024]{1,0:T(8,128)(2,1)}, bf16[2048,1024]{1,0:T(8,128)(2,1)}, f32[2048,8]{1,0:T(8,128)}, bf16[2080,128]{1,0:T(8,128)(2,1)}) custom-call(bf16[1024,1024]{1,0:T(8,128)(2,1)} %convolution_convert_fusion.11.dg0_ref, bf16[1024,1024]{1,0:T(8,128)(2,1)} %convolution_convert_fusion.10.dg1_ref, ...), custom_call_target="tpu_custom_call" | custom-call | tf_op jit(solution)/shard_map/pallas_call | solution.py:68
  343.7 4.6 convolution_convert_fusion.7
  359.7 17.4 %shard_map.184 = (bf16[2048,1024]{1,0:T(8,128)(2,1)}, f32[32,1024]{1,0:T(8,128)}, f32[256,1024]{1,0:T(8,128)}) custom-call(bf16[2048,1024]{1,0:T(8,128)(2,1)} %get-tuple-element.103.xs_ref, bf16[2048,1024]{1,0:T(8,128)(2,1)} %get-tuple-element.122.dy_ref, bf16[256,1024]{1,0:T(8,128)(2,1)} %get-tuple-element.104.bc_ref, ...), custom_call_target="tpu_custom_call" | custom-call | flops 6442450944 | bytes 12582912 | tf_op jit(solution)/shard_map/pallas_call | solution.py:68
  377.1 4.4 fusion.68
  385.3 7.1 fusion
  392.4 36.5 %shard_map.185 = (bf16[2336,1024]{1,0:T(8,128)(2,1)}, f32[8,2304]{1,0:T(8,128)}, f32[2304,8]{1,0:T(8,128)}, f32[32,8]{1,0:T(8,128)}) custom-call(bf16[2336,1152]{1,0:T(8,128)(2,1)} %convolution_convert_fusion.u_ref.halo_ref.step_ref, bf16[2336,1152]{1,0:T(8,128)(2,1)} %convolution_convert_fusion.u_ref.halo_ref.step_ref, ...), custom_call_target="tpu_custom_call" | custom-call | flops 2684354560 | bytes 38797312 | tf_op jit(solution)/shard_map/pallas_call | solution.py:68
  430.3 8.6 %fusion.10 = f32[1024,1024]{1,0:T(8,128)} fusion(bf16[2048,1024]{1,0:T(8,128)(2,1)S(1)} %copy-done.54, bf16[1024,4384]{1,0:T(8,128)(2,1)} %all-gather.6.cloned.1.call-done), kind=kOutput, calls=%fused_computation.40 | convolution fusion | flops 4294967296 | bytes 12582912 | tf_op jit(solution)/shard_map/dot_general | solution.py:22
  439.5 4.9 shard_map.186
  444.4 5.5 convolution_convert_fusion.3
  460.3 6.7 all-to-all-start
  467.0 11.7 %multiply_reduce_fusion = (f32[1024]{0:T(1024)S(1)}, f32[1024]{0:T(1024)S(1)}, f32[1024,1024]{1,0:T(8,128)S(1)}) fusion(f32[1024,1024]{1,0:T(8,128)} %copy-done.2, f32[1024]{0:T(1024)S(1)} %add_rsqrt_fusion, f32[1024]{0:T(1024)S(1)} %slice.354, f32[1024,1024]{1,0:T(8,128)} %fusion.10, bf16[2336,1024]{1,0:T(8,128)(2,1)} %shard_map.186, ...), kind=kOutput, calls=%fused_computation.24 | convolution fusion | flops 4906285056 | bytes 22364160 | tf_op jit(solution)/shard_map/dot_general | solution.py:22
  481.4 11.1 %reduce-scatter.2.cloned.1.call-done = bf16[32,4096]{1,0:T(8,128)(2,1)} async-done(((bf16[512,4096]{1,0:T(8,128)(2,1)}), bf16[32,4096]{1,0:T(8,128)(2,1)}) %reduce-scatter.2.cloned.1.call-update) | async-done | bytes 262160 | tf_op jit(solution)/shard_map/reduce_scatter | solution.py:875
  497.0 5.3 convolution_convert_fusion.8.dg1_ref
  502.3 5.3 convolution_convert_fusion.9.dg0_ref
  507.6 17.0 %shard_map.187 = (bf16[2048,1024]{1,0:T(8,128)(2,1)}, bf16[2048,1024]{1,0:T(8,128)(2,1)}, f32[2048,8]{1,0:T(8,128)}, bf16[2080,128]{1,0:T(8,128)(2,1)}) custom-call(bf16[1024,1024]{1,0:T(8,128)(2,1)} %convolution_convert_fusion.9.dg0_ref, bf16[1024,1024]{1,0:T(8,128)(2,1)} %convolution_convert_fusion.8.dg1_ref, ...), custom_call_target="tpu_custom_call" | custom-call | tf_op jit(solution)/shard_map/pallas_call | solution.py:68
  524.6 4.7 convolution_convert_fusion.6
  544.8 17.4 %shard_map.188 = (bf16[2048,1024]{1,0:T(8,128)(2,1)}, f32[32,1024]{1,0:T(8,128)}, f32[256,1024]{1,0:T(8,128)}) custom-call(bf16[2048,1024]{1,0:T(8,128)(2,1)} %get-tuple-element.90.xs_ref, bf16[2048,1024]{1,0:T(8,128)(2,1)} %get-tuple-element.143.dy_ref, bf16[256,1024]{1,0:T(8,128)(2,1)} %get-tuple-element.91.bc_ref, f32[32,1024]{1,0:T(8,128)} %get-tuple-element.92.dt_ref, ...), custom_call_target="tpu_custom_call" | custom-call | flops 6442450944 | bytes 12582912 | tf_op jit(solution)/shard_map/pallas_call | solution.py:68
  563.0 3.8 fusion.59
  570.4 4.3 fusion.57
  579.2 6.0 fusion.1
  585.2 7.8 %all-to-all-start.2 = ((bf16[4,128,4096]{2,1,0:T(8,128)(2,1)}), bf16[4,128,4096]{2,1,0:T(8,128)(2,1)}, u32[]{:S(2)}, u32[]{:S(2)}) async-start(bf16[4,128,4096]{2,1,0:T(8,128)(2,1)} %bitcast.195), calls=%async_computation.3 | async-start | bytes 8388608 | tf_op jit(solution)/shard_map/all_to_all | solution.py:863
  593.1 36.4 %shard_map.189 = (bf16[2336,1024]{1,0:T(8,128)(2,1)}, f32[8,2304]{1,0:T(8,128)}, f32[2304,8]{1,0:T(8,128)}, f32[32,8]{1,0:T(8,128)}) custom-call(bf16[2336,1152]{1,0:T(8,128)(2,1)} %convolution_convert_fusion.1.u_ref.halo_ref.step_ref, bf16[2336,1152]{1,0:T(8,128)(2,1)} %convolution_convert_fusion.1.u_ref.halo_ref.step_ref, ...), custom_call_target="tpu_custom_call" | custom-call | flops 2684354560 | bytes 38797312 | tf_op jit(solution)/shard_map/pallas_call | solution.py:68
  629.5 8.3 %fusion.13 = f32[1024,1024]{1,0:T(8,128)} fusion(bf16[2048,1024]{1,0:T(8,128)(2,1)S(1)} %copy-done.52, bf16[1024,6432]{1,0:T(8,128)(2,1)} %all-gather.4.cloned.1.call-done), kind=kOutput, calls=%fused_computation.43 | convolution fusion | flops 4294967296 | bytes 12582912 | tf_op jit(solution)/shard_map/dot_general | solution.py:22
  640.7 4.2 reduce_sum.150
  644.9 4.8 all-to-all-start.3
  651.4 5.0 collective-permute-done.21.ahead_ref
  657.1 4.8 shard_map.190
  661.8 6.5 convolution_convert_fusion.2
  668.3 5.8 all-to-all-done.3
  674.4 4.3 collective-permute-start.23
  684.5 6.1 fusion.3
  692.5 4.7 all-to-all-start.4
  697.2 12.8 %multiply_reduce_fusion.1 = (f32[1024]{0:T(1024)S(1)}, f32[1024]{0:T(1024)S(1)}, f32[1024,1024]{1,0:T(8,128)}) fusion(f32[1024,1024]{1,0:T(8,128)} %copy-done, f32[1024]{0:T(1024)S(1)} %copy-done.35, f32[1024]{0:T(1024)S(1)} %copy-done.31, f32[1024,1024]{1,0:T(8,128)} %fusion.13, bf16[2336,1024]{1,0:T(8,128)(2,1)} %shard_map.190, ...), kind=kOutput, calls=%fused_computation.25 | convolution fusion | flops 4906285056 | bytes 22364160 | tf_op jit(solution)/shard_map/dot_general | solution.py:22
  713.8 11.2 %collective-permute-done.26 = f32[14688]{0:T(1024)S(1)} collective-permute-done((f32[14688]{0:T(1024)S(1)}, f32[14688]{0:T(1024)S(1)}, u32[]{:S(2)}, u32[]{:S(2)}) %collective-permute-start.26) | collective-permute-done | bytes 58784 | tf_op jit(solution)/shard_map/ppermute | solution.py:782
  729.4 4.7 collective-permute-done.28
  739.3 4.1 all-to-all-start.5
  743.4 7.8 %select_bitcast_fusion.1 = (f32[1,1024,1024]{2,1,0:T(8,128)}, f32[1024,1024]{1,0:T(8,128)}) fusion(f32[1024,1024]{1,0:T(8,128)} %collective-permute-done.23, pred[]{:T(512)S(6)} %eq.4, f32[1024,1024]{1,0:T(8,128)} %get-tuple-element.225, f32[1024,1024]{1,0:T(8,128)} %copy-done, f32[1024]{0:T(1024)S(1)} %fusion.101, f32[1024,1024]{1,0:T(8,128)} %get-tuple-element.261, ...), kind=kLoop, calls=%fused_computation.27 | loop fusion | flops 6291456 | bytes 25178112 | tf_op jit(solution)/shard_map/stack | solution.py:1061
  767.9 4.2 maximum_bitcast_fusion
  (336 shorter events, 158.3 us)
Async XLA Ops:
  7.2 108.4 %all-gather.4.cloned.1.call-start = ((), (), s32[]{:S(2)}) async-start(), calls=%async_computation.7 | async-start | bytes 13787136 | tf_op jit(solution)/shard_map/all_gather | solution.py:822
  9.7 1.9 collective-permute-start.1
  12.5 200.1 %all-gather.6.cloned.1.call-start = ((), (), s32[]{:S(2)}) async-start(), calls=%async_computation.8 | async-start | bytes 9461760 | tf_op jit(solution)/shard_map/all_gather | solution.py:822
  13.4 289.1 %all-gather.8.cloned.1.call-start = ((), (), s32[]{:S(2)}) async-start(), calls=%async_computation.9 | async-start | bytes 4325376 | tf_op jit(solution)/shard_map/all_gather | solution.py:822
  20.3 11.2 %collective-permute-start = (f32[1024,1024]{1,0:T(8,128)}, f32[1024,1024]{1,0:T(8,128)}, u32[]{:S(2)}, u32[]{:S(2)}) collective-permute-start(f32[1024,1024]{1,0:T(8,128)} %bitcast_select_fusion.1), channel_id=1, source_target_pairs={{0,16},{16,0},{1,17},{17,1},{2,18},{18,2},{3,19},{19,3},{4,20},{20... | collective-permute-start | bytes 12582920 | tf_op jit(solution)/shard_map/ppermute | solution.py:770
  20.9 6.5 collective-permute-start.2
  27.6 31.6 %copy-start.30 = (f32[1024]{0:T(1024)}, f32[1024]{0:T(1024)S(1)}, u32[]{:S(2)}) copy-start(f32[1024]{0:T(1024)S(1)} %slice.337) | copy-start | bytes 12292
  39.0 13.9 %copy-start = (f32[1024,1024]{1,0:T(8,128)}, f32[1024,1024]{1,0:T(8,128)S(1)}, u32[]{:S(2)}) copy-start(f32[1024,1024]{1,0:T(8,128)S(1)} %get-tuple-element.227) | copy-start | bytes 12582916
  39.0 13.9 %copy-start.36 = (f32[1024]{0:T(1024)}, f32[1024]{0:T(1024)S(1)}, u32[]{:S(2)}) copy-start(f32[1024]{0:T(1024)S(1)} %get-tuple-element.226) | copy-start | bytes 12292
  46.3 12.7 %collective-permute-start.3 = (f32[8,1024]{1,0:T(8,128)S(1)}, f32[8,1024]{1,0:T(8,128)S(1)}, u32[]{:S(2)}, u32[]{:S(2)}) collective-permute-start(f32[8,1024]{1,0:T(8,128)S(1)} %slice.338), channel_id=1, source_target_pairs={{0,1},{1,2},{2,3},{4,5},{5,6},{6,7},{8,9},{9,10},{10,11},{12,13},{... | collective-permute-start | bytes 98312 | tf_op jit(solution)/shard_map/ppermute | solution.py:764
  128.0 24.9 %copy-start.18 = (bf16[1024,1024]{1,0:T(8,128)(2,1)S(1)}, bf16[1024,1024]{1,0:T(8,128)(2,1)}, u32[]{:S(2)}) copy-start(bf16[1024,1024]{1,0:T(8,128)(2,1)} %multiply_convert_fusion.1) | copy-start | bytes 6291460
  145.1 28.1 %collective-permute-start.6 = (bf16[2080,128]{1,0:T(8,128)(2,1)}, bf16[2080,128]{1,0:T(8,128)(2,1)}, u32[]{:S(2)}, u32[]{:S(2)}) collective-permute-start(bf16[2080,128]{1,0:T(8,128)(2,1)} %get-tuple-element.97), channel_id=1, source_target_pairs={{0,3},{4,7},{8,11},{12,15},{16,19},{20,23},{24,27},{28,31}} | collective-permute-start | bytes 1597448 | tf_op jit(solution)/shard_map/ppermute | solution.py:764
  149.3 31.0 %collective-permute-start.5 = (bf16[2080,128]{1,0:T(8,128)(2,1)}, bf16[2080,128]{1,0:T(8,128)(2,1)S(1)}, u32[]{:S(2)}, u32[]{:S(2)}) collective-permute-start(bf16[2080,128]{1,0:T(8,128)(2,1)} %get-tuple-element.97), channel_id=1, source_target_pairs={{0,2},{1,3},{4,6},{5,7},{8,10},{9,11},{12,14},{13,15},{16,18},{17,... | collective-permute-start | bytes 1597448 | tf_op jit(solution)/shard_map/ppermute | solution.py:764
  150.6 29.8 %collective-permute-start.4 = (bf16[2080,128]{1,0:T(8,128)(2,1)}, bf16[2080,128]{1,0:T(8,128)(2,1)S(1)}, u32[]{:S(2)}, u32[]{:S(2)}) collective-permute-start(bf16[2080,128]{1,0:T(8,128)(2,1)} %get-tuple-element.97), channel_id=1, source_target_pairs={{0,1},{1,2},{2,3},{4,5},{5,6},{6,7},{8,9},{9,10},{10,11},{12,13},{... | collective-permute-start | bytes 1597448 | tf_op jit(solution)/shard_map/ppermute | solution.py:764
  152.3 340.2 %reduce-scatter.2.cloned.1.call-start = ((), (), s32[]{:S(2)}) async-start(), calls=%async_computation.10 | async-start | bytes 4456448 | tf_op jit(solution)/shard_map/reduce_scatter | solution.py:875
  207.5 13.8 %copy-start.39 = (f32[1024]{0:T(1024)}, f32[1024]{0:T(1024)S(1)}, u32[]{:S(2)}) copy-start(f32[1024]{0:T(1024)S(1)} %get-tuple-element.258) | copy-start | bytes 12292
  207.5 13.8 %collective-permute-start.7 = (f32[8,1024]{1,0:T(8,128)S(1)}, f32[8,1024]{1,0:T(8,128)S(1)}, u32[]{:S(2)}, u32[]{:S(2)}) collective-permute-start(f32[8,1024]{1,0:T(8,128)S(1)} %slice.355), channel_id=1, source_target_pairs={{0,1},{1,2},{2,3},{4,5},{5,6},{6,7},{8,9},{9,10},{10,11},{12,13},{... | collective-permute-start | bytes 98312 | tf_op jit(solution)/shard_map/ppermute | solution.py:764
  230.7 23.2 %copy-start.3 = (f32[1024,1024]{1,0:T(8,128)S(1)}, f32[1024,1024]{1,0:T(8,128)}, u32[]{:S(2)}) copy-start(f32[1024,1024]{1,0:T(8,128)} %copy-done.2) | copy-start | bytes 12582916
  247.8 25.1 %collective-permute-start.10 = (bf16[2080,128]{1,0:T(8,128)(2,1)}, bf16[2080,128]{1,0:T(8,128)(2,1)}, u32[]{:S(2)}, u32[]{:S(2)}) collective-permute-start(bf16[2080,128]{1,0:T(8,128)(2,1)} %get-tuple-element.110), channel_id=1, source_target_pairs={{0,3},{4,7},{8,11},{12,15},{16,19},{20,23},{24,27},{28,31}} | collective-permute-start | bytes 1597448 | tf_op jit(solution)/shard_map/ppermute | solution.py:764
  250.0 30.7 %collective-permute-start.9 = (bf16[2080,128]{1,0:T(8,128)(2,1)}, bf16[2080,128]{1,0:T(8,128)(2,1)S(1)}, u32[]{:S(2)}, u32[]{:S(2)}) collective-permute-start(bf16[2080,128]{1,0:T(8,128)(2,1)} %get-tuple-element.110), channel_id=1, source_target_pairs={{0,2},{1,3},{4,6},{5,7},{8,10},{9,11},{12,14},{13,15},{16,18},{17,... | collective-permute-start | bytes 1597448 | tf_op jit(solution)/shard_map/ppermute | solution.py:764
  251.3 29.4 %collective-permute-start.8 = (bf16[2080,128]{1,0:T(8,128)(2,1)}, bf16[2080,128]{1,0:T(8,128)(2,1)S(1)}, u32[]{:S(2)}, u32[]{:S(2)}) collective-permute-start(bf16[2080,128]{1,0:T(8,128)(2,1)} %get-tuple-element.110), channel_id=1, source_target_pairs={{0,1},{1,2},{2,3},{4,5},{5,6},{6,7},{8,9},{9,10},{10,11},{12,13},{... | collective-permute-start | bytes 1597448 | tf_op jit(solution)/shard_map/ppermute | solution.py:764
  302.5 14.2 %copy-start.21 = (bf16[2,1,512,1024]{3,2,1,0:T(8,128)(2,1)}, bf16[2,1,512,1024]{3,2,1,0:T(8,128)(2,1)S(1)}, u32[]{:S(2)}) copy-start(bf16[2,1,512,1024]{3,2,1,0:T(8,128)(2,1)S(1)} %get-tuple-element.232) | copy-start | bytes 6291460
  326.3 17.4 %copy-start.17 = (bf16[2,1,4,4,32,1024]{5,4,3,2,0,1:T(8,128)(2,1)S(1)}, bf16[2,1,4,4,32,1024]{5,4,3,2,0,1:T(8,128)(2,1)}, u32[]{:S(2)}) copy-start(bf16[2,1,4,4,32,1024]{5,4,3,2,0,1:T(8,128)(2,1)} %copy.90) | copy-start | bytes 6291460
  350.5 34.8 %collective-permute-start.11 = (bf16[512,4096]{1,0:T(8,128)(2,1)}, bf16[512,4096]{1,0:T(8,128)(2,1)}, u32[]{:S(2)}, u32[]{:S(2)}) collective-permute-start(bf16[512,4096]{1,0:T(8,128)(2,1)} %pad_maximum_fusion), channel_id=1, source_target_pairs={{0,16},{16,0},{1,17},{17,1},{2,18},{18,2},{3,19},{19,3},{4,20},{20... | collective-permute-start | bytes 12582920 | tf_op jit(solution)/shard_map/ppermute | solution.py:770
  350.5 31.0 %collective-permute-start.14 = (bf16[2080,128]{1,0:T(8,128)(2,1)}, bf16[2080,128]{1,0:T(8,128)(2,1)S(1)}, u32[]{:S(2)}, u32[]{:S(2)}) collective-permute-start(bf16[2080,128]{1,0:T(8,128)(2,1)} %get-tuple-element.127), channel_id=1, source_target_pairs={{3,0},{7,4},{11,8},{15,12},{19,16},{23,20},{27,24},{31,28}} | collective-permute-start | bytes 1597448 | tf_op jit(solution)/shard_map/ppermute | solution.py:764
  351.9 29.6 %collective-permute-start.13 = (bf16[2080,128]{1,0:T(8,128)(2,1)}, bf16[2080,128]{1,0:T(8,128)(2,1)S(1)}, u32[]{:S(2)}, u32[]{:S(2)}) collective-permute-start(bf16[2080,128]{1,0:T(8,128)(2,1)} %get-tuple-element.127), channel_id=1, source_target_pairs={{2,0},{3,1},{6,4},{7,5},{10,8},{11,9},{14,12},{15,13},{18,16},{19,... | collective-permute-start | bytes 1597448 | tf_op jit(solution)/shard_map/ppermute | solution.py:764
  353.2 28.3 %collective-permute-start.12 = (bf16[2080,128]{1,0:T(8,128)(2,1)}, bf16[2080,128]{1,0:T(8,128)(2,1)S(1)}, u32[]{:S(2)}, u32[]{:S(2)}) collective-permute-start(bf16[2080,128]{1,0:T(8,128)(2,1)} %get-tuple-element.127), channel_id=1, source_target_pairs={{1,0},{2,1},{3,2},{5,4},{6,5},{7,6},{9,8},{10,9},{11,10},{13,12},{... | collective-permute-start | bytes 1597448 | tf_op jit(solution)/shard_map/ppermute | solution.py:764
  359.7 17.4 %copy-start.53 = (bf16[2048,1024]{1,0:T(8,128)(2,1)S(1)}, bf16[2048,1024]{1,0:T(8,128)(2,1)}, u32[]{:S(2)}) copy-start(bf16[2048,1024]{1,0:T(8,128)(2,1)} %get-tuple-element.132) | copy-start | bytes 12582916
  392.4 37.9 %copy-start.54 = (bf16[2048,1024]{1,0:T(8,128)(2,1)S(1)}, bf16[2048,1024]{1,0:T(8,128)(2,1)}, u32[]{:S(2)}) copy-start(bf16[2048,1024]{1,0:T(8,128)(2,1)} %get-tuple-element.132) | copy-start | bytes 12582916
  429.0 10.0 %collective-permute-start.15 = (f32[8,2304]{1,0:T(8,128)}, f32[8,2304]{1,0:T(8,128)S(1)}, u32[]{:S(2)}, u32[]{:S(2)}) collective-permute-start(f32[8,2304]{1,0:T(8,128)} %get-tuple-element.131), channel_id=1, source_target_pairs={{1,0},{2,1},{3,2},{5,4},{6,5},{7,6},{9,8},{10,9},{11,10},{13,12},{... | collective-permute-start | bytes 221192 | tf_op jit(solution)/shard_map/ppermute | solution.py:764
  449.9 4.7 collective-permute-start.16
  460.3 72.7 %all-to-all-start = ((bf16[4,128,2336]{1,2,0:T(8,128)(2,1)}), bf16[4,128,2336]{1,2,0:T(8,128)(2,1)}, u32[]{:S(2)}, u32[]{:S(2)}) async-start(bf16[4,128,2336]{1,2,0:T(8,128)(2,1)} %copy_bitcast_fusion.1), calls=%async_computation.1 | async-start | bytes 4784128 | tf_op jit(solution)/shard_map/all_to_all | solution.py:863
  467.0 11.8 %copy-start.40 = (f32[1024]{0:T(1024)S(1)}, f32[1024]{0:T(1024)}, u32[]{:S(2)}) copy-start(f32[1024]{0:T(1024)} %copy-done.39) | copy-start | bytes 12292
  467.0 11.8 %copy-start.5 = (f32[1024,1024]{1,0:T(8,128)S(1)}, f32[1024,1024]{1,0:T(8,128)}, u32[]{:S(2)}) copy-start(f32[1024,1024]{1,0:T(8,128)} %copy-done.2) | copy-start | bytes 12582916
  467.0 11.8 %copy-start.7 = (f32[1024,1024]{1,0:T(8,128)S(1)}, f32[1024,1024]{1,0:T(8,128)}, u32[]{:S(2)}) copy-start(f32[1024,1024]{1,0:T(8,128)} %get-tuple-element.116) | copy-start | bytes 12582916
  481.4 47.9 %copy-start.12 = (bf16[1024,1024]{1,0:T(8,128)(2,1)}, bf16[1024,1024]{1,0:T(8,128)(2,1)S(1)}, u32[]{:S(2)}) copy-start(bf16[1024,1024]{1,0:T(8,128)(2,1)S(1)} %get-tuple-element.136) | copy-start | bytes 6291460
  507.6 17.0 %copy-start.14 = (bf16[2,1,4,4,32,1024]{5,4,3,2,0,1:T(8,128)(2,1)S(1)}, bf16[2,1,4,4,32,1024]{5,4,3,2,0,1:T(8,128)(2,1)}, u32[]{:S(2)}) copy-start(bf16[2,1,4,4,32,1024]{5,4,3,2,0,1:T(8,128)(2,1)} %copy.88) | copy-start | bytes 6291460
  532.9 46.3 %collective-permute-start.17 = (bf16[512,4096]{1,0:T(8,128)(2,1)}, bf16[512,4096]{1,0:T(8,128)(2,1)}, u32[]{:S(2)}, u32[]{:S(2)}) collective-permute-start(bf16[512,4096]{1,0:T(8,128)(2,1)} %pad_maximum_fusion.1), channel_id=1, source_target_pairs={{0,16},{16,0},{1,17},{17,1},{2,18},{18,2},{3,19},{19,3},{4,20},{20... | collective-permute-start | bytes 12582920 | tf_op jit(solution)/shard_map/ppermute | solution.py:770
  537.4 24.7 %all-to-all-start.1 = ((bf16[4,32,2336]{2,1,0:T(8,128)(2,1)}), bf16[4,32,2336]{2,1,0:T(8,128)(2,1)S(1)}, u32[]{:S(2)}, u32[]{:S(2)}) async-start(bf16[4,32,2336]{2,1,0:T(8,128)(2,1)} %bitcast.201), calls=%async_computation.2 | async-start | bytes 1245184 | tf_op jit(solution)/shard_map/all_to_all | solution.py:870
  540.9 33.8 %collective-permute-start.20 = (bf16[2080,128]{1,0:T(8,128)(2,1)}, bf16[2080,128]{1,0:T(8,128)(2,1)}, u32[]{:S(2)}, u32[]{:S(2)}) collective-permute-start(bf16[2080,128]{1,0:T(8,128)(2,1)} %get-tuple-element.148), channel_id=1, source_target_pairs={{3,0},{7,4},{11,8},{15,12},{19,16},{23,20},{27,24},{31,28}} | collective-permute-start | bytes 1597448 | tf_op jit(solution)/shard_map/ppermute | solution.py:764
  542.2 32.5 %collective-permute-start.19 = (bf16[2080,128]{1,0:T(8,128)(2,1)}, bf16[2080,128]{1,0:T(8,128)(2,1)}, u32[]{:S(2)}, u32[]{:S(2)}) collective-permute-start(bf16[2080,128]{1,0:T(8,128)(2,1)} %get-tuple-element.148), channel_id=1, source_target_pairs={{2,0},{3,1},{6,4},{7,5},{10,8},{11,9},{14,12},{15,13},{18,16},{19,... | collective-permute-start | bytes 1597448 | tf_op jit(solution)/shard_map/ppermute | solution.py:764
  543.5 31.2 %collective-permute-start.18 = (bf16[2080,128]{1,0:T(8,128)(2,1)}, bf16[2080,128]{1,0:T(8,128)(2,1)}, u32[]{:S(2)}, u32[]{:S(2)}) collective-permute-start(bf16[2080,128]{1,0:T(8,128)(2,1)} %get-tuple-element.148), channel_id=1, source_target_pairs={{1,0},{2,1},{3,2},{5,4},{6,5},{7,6},{9,8},{10,9},{11,10},{13,12},{... | collective-permute-start | bytes 1597448 | tf_op jit(solution)/shard_map/ppermute | solution.py:764
  544.8 18.2 %copy-start.13 = (bf16[1024,1024]{1,0:T(8,128)(2,1)S(1)}, bf16[1024,1024]{1,0:T(8,128)(2,1)}, u32[]{:S(2)}) copy-start(bf16[1024,1024]{1,0:T(8,128)(2,1)} %copy-done.12) | copy-start | bytes 6291460
  585.2 55.5 %all-to-all-start.2 = ((bf16[4,128,4096]{2,1,0:T(8,128)(2,1)}), bf16[4,128,4096]{2,1,0:T(8,128)(2,1)}, u32[]{:S(2)}, u32[]{:S(2)}) async-start(bf16[4,128,4096]{2,1,0:T(8,128)(2,1)} %bitcast.195), calls=%async_computation.3 | async-start | bytes 8388608 | tf_op jit(solution)/shard_map/all_to_all | solution.py:863
  593.1 36.4 %copy-start.52 = (bf16[2048,1024]{1,0:T(8,128)(2,1)S(1)}, bf16[2048,1024]{1,0:T(8,128)(2,1)}, u32[]{:S(2)}) copy-start(bf16[2048,1024]{1,0:T(8,128)(2,1)} %get-tuple-element.153) | copy-start | bytes 12582916
  637.8 11.8 %copy-start.57 = (f32[8,2304]{1,0:T(8,128)S(1)}, f32[8,2304]{1,0:T(8,128)}, u32[]{:S(2)}) copy-start(f32[8,2304]{1,0:T(8,128)} %get-tuple-element.152) | copy-start | bytes 221188
  644.9 29.2 %all-to-all-start.3 = ((bf16[4,32,4096]{2,1,0:T(8,128)(2,1)}), bf16[4,32,4096]{2,1,0:T(8,128)(2,1)S(1)}, u32[]{:S(2)}, u32[]{:S(2)}) async-start(bf16[4,32,4096]{2,1,0:T(8,128)(2,1)} %bitcast.46), calls=%async_computation.4 | async-start | bytes 2097152 | tf_op jit(solution)/shard_map/all_to_all | solution.py:870
  649.7 6.8 collective-permute-start.21
  661.8 18.4 %copy-start.41 = (f32[32,8]{1,0:T(8,128)S(1)}, f32[32,8]{1,0:T(8,128)}, u32[]{:S(2)}) copy-start(f32[32,8]{1,0:T(8,128)} %get-tuple-element.165) | copy-start | bytes 3076
  661.8 18.6 %copy-start.26 = (f32[2304,8]{1,0:T(8,128)S(1)}, f32[2304,8]{1,0:T(8,128)}, u32[]{:S(2)}) copy-start(f32[2304,8]{1,0:T(8,128)} %get-tuple-element.164) | copy-start | bytes 221188
  668.3 14.3 %copy-start.42 = (f32[32,8]{1,0:T(8,128)S(1)}, f32[32,8]{1,0:T(8,128)}, u32[]{:S(2)}) copy-start(f32[32,8]{1,0:T(8,128)} %get-tuple-element.162) | copy-start | bytes 3076
  674.3 10.2 %collective-permute-start.22 = (bf16[512,2336]{0,1:T(8,128)(2,1)}, bf16[512,2336]{0,1:T(8,128)(2,1)}, u32[]{:S(2)}, u32[]{:S(2)}) collective-permute-start(bf16[512,2336]{0,1:T(8,128)(2,1)} %convolution_convert_fusion.2), channel_id=1, source_target_pairs={{0,16},{16,0},{1,17},{17,1},{2,18},{18,2},{3,19},{19,3},{4,20},{20... | collective-permute-start | bytes 7176200 | tf_op jit(solution)/shard_map/ppermute | solution.py:770
  674.4 69.0 %collective-permute-start.23 = (f32[1024,1024]{1,0:T(8,128)}, f32[1024,1024]{1,0:T(8,128)}, u32[]{:S(2)}, u32[]{:S(2)}) collective-permute-start(f32[1024,1024]{1,0:T(8,128)} %add_add_fusion), channel_id=1, source_target_pairs={{0,16},{1,17},{2,18},{3,19},{4,20},{5,21},{6,22},{7,23},{8,24},{9,... | collective-permute-start | bytes 12582920 | tf_op jit(solution)/shard_map/ppermute | solution.py:1053
  692.5 42.3 %all-to-all-start.4 = ((bf16[4,128,2336]{1,2,0:T(8,128)(2,1)}), bf16[4,128,2336]{1,2,0:T(8,128)(2,1)}, u32[]{:S(2)}, u32[]{:S(2)}) async-start(bf16[4,128,2336]{1,2,0:T(8,128)(2,1)} %copy_bitcast_fusion), calls=%async_computation.5 | async-start | bytes 4784128 | tf_op jit(solution)/shard_map/all_to_all | solution.py:863
  697.2 32.2 %copy-start.37 = (f32[1024]{0:T(1024)S(1)}, f32[1024]{0:T(1024)}, u32[]{:S(2)}) copy-start(f32[1024]{0:T(1024)} %copy-done.36) | copy-start | bytes 12292
  710.1 1.3 collective-permute-start.25
  711.4 13.6 %collective-permute-start.26 = (f32[14688]{0:T(1024)S(1)}, f32[14688]{0:T(1024)S(1)}, u32[]{:S(2)}, u32[]{:S(2)}) collective-permute-start(f32[14688]{0:T(1024)S(1)} %select_add_fusion), channel_id=1, source_target_pairs={{0,1},{1,0},{2,3},{3,2},{4,5},{5,4},{6,7},{7,6},{8,9},{9,8},{10,11... | collective-permute-start | bytes 176264 | tf_op jit(solution)/shard_map/ppermute | solution.py:782
  725.0 4.3 collective-permute-start.27
  729.3 4.8 collective-permute-start.28
  734.7 17.7 %collective-permute-start.29 = (f32[14688]{0:T(1024)}, f32[14688]{0:T(1024)}, u32[]{:S(2)}, u32[]{:S(2)}) collective-permute-start(f32[14688]{0:T(1024)} %add.179), channel_id=1, source_target_pairs={{0,8},{4,12},{8,0},{12,4},{1,9},{5,13},{9,1},{13,5},{2,10},{6,14},... | collective-permute-start | bytes 176264 | tf_op jit(solution)/shard_map/ppermute | solution.py:782
  739.3 17.2 %all-to-all-start.5 = ((bf16[4,32,2336]{2,1,0:T(8,128)(2,1)}), bf16[4,32,2336]{2,1,0:T(8,128)(2,1)S(1)}, u32[]{:S(2)}, u32[]{:S(2)}) async-start(bf16[4,32,2336]{2,1,0:T(8,128)(2,1)} %bitcast.200), calls=%async_computation.6 | async-start | bytes 1245184 | tf_op jit(solution)/shard_map/all_to_all | solution.py:870
  743.4 13.2 %copy-start.11 = (f32[32,2336]{1,0:T(8,128)S(1)}, f32[32,2336]{1,0:T(8,128)}, u32[]{:S(2)}) copy-start(f32[32,2336]{1,0:T(8,128)} %convert_reduce_fusion.2) | copy-start | bytes 897028
  751.2 13.3 %collective-permute-start.24 = (f32[1024,1024]{1,0:T(8,128)}, f32[1024,1024]{1,0:T(8,128)}, u32[]{:S(2)}, u32[]{:S(2)}) collective-permute-start(f32[1024,1024]{1,0:T(8,128)} %get-tuple-element.223), channel_id=1, source_target_pairs={{16,0},{17,1},{18,2},{19,3},{20,4},{21,5},{22,6},{23,7},{24,8},{25... | collective-permute-start | bytes 12582920 | tf_op jit(solution)/shard_map/ppermute | solution.py:1059
  756.7 5.1 collective-permute-start.30
  (35 other events, 186.4 us)
Sparse Core Ops, SparseCore 0:
  12.7 102.8 all-gather.3
  118.4 81.7 all-gather.5
  203.1 72.8 all-gather.7
  392.5 99.9 reduce-scatter.1
where the time goes:
time: 786 us; the launch traced here: 779 us
  Pallas kernels  239 us (30%)
  matrix products  176 us (22%)
  waiting for transfers between devices  127 us (16%)
  other arithmetic  83.9 us (11%)
  starting transfers between devices  79.6 us (10%)
  local copies, waits for them, and re-layouts  58.3 us (7%)
  between operations  15.3 us (2%)
    pallas_call x12, Pallas kernels, call(): pl.pallas_call(kernel, grid=grid, in_specs=[s for _, s in ins], out_specs...  229 us
    dot_general x32, matrix products, contract(): lax.dot_general(a, b, (((a_dim,), (b_dim,)), ((), ())), preferred_element...  176 us
    all_gather x3, waiting for transfers between devices, gathered(): everyone = lambda a: lax.all_gather(a, across, axis=0, tiled=True)  56.4 us
    ppermute x16, starting transfers between devices, shifted(): lax.ppermute(x, axis, [(i, i + by) for i in range(devices) if 0 <= i + by...  33.5 us
    ppermute x16, waiting for transfers between devices, shifted(): lax.ppermute(x, axis, [(i, i + by) for i in range(devices) if 0 <= i + by...  19.9 us
    ppermute x4, waiting for transfers between devices, summed(): value = value + lax.ppermute(value, axis, pairs)  19.2 us
    all_to_all x3, starting transfers between devices, over_head(): lax.all_to_all(part, 'head', split_axis=0, concat_axis=0, tiled=True)  19.2 us
  transfers between devices with their start and end apart: 41, of which 15 were waited for; matrix products, arithmetic and copies ran while one was open for 33% of the time, Pallas kernels for 28%

commit v1 on v0

--- a/solution.py
+++ b/solution.py
@@ -405,7 +405,9 @@
     def _():
         send_ref[:inner, :] = ds[...].astype(LOW)
         send_ref[inner:, :] = decays_ref[...]
-        gsum_ref[:, 0:1] = jnp.sum(gg[...], axis=1, keepdims=True)
+        for at in range(0, inner, BLOCK):
+            rows = slice(at, at + BLOCK)
+            gsum_ref[0:1, rows] = column_sum(gg[rows, :].T)
 
 
 def gate_backward(dg0, dg1, ylow, z, bc, wt, gain, decays):
@@ -422,7 +424,7 @@
         [
             token_out(inner, length, LOW),
             token_out(inner, length, LOW),
-            fixed_out((inner, 8), F32),
+            fixed_out((8, inner), F32),
             fixed_out((inner + heads, n_state), LOW),
         ],
         [
@@ -633,10 +635,8 @@
     def _():
         first_ref[...] = dc_first[...].T[: first_ref.shape[0], :]
         lane = lax.broadcasted_iota(jnp.int32, (1, BLOCK), 1)
-        size = channels // 8
-
-        def sums(i, carry):
-            rows = pl.ds(pl.multiple_of(i * size, 16), size)
+        for at in range(0, channels, BLOCK):
+            rows = slice(at, at + BLOCK)
             halo = halo_ref[rows, :].astype(F32)
             dc = dc_first[rows, :]
             for k in range(taps + 1):
@@ -644,10 +644,7 @@
                 if k < taps - 1:
                     back = taps - 1 - k
                     total = total + jnp.where(lane < back, pltpu.roll(halo, back, 1) * dc, 0.0)
-                csum_ref[rows, k : k + 1] = jnp.sum(total, axis=1, keepdims=True)
-            return carry
-
-        lax.fori_loop(0, 8, sums, 0)
+                csum_ref[k : k + 1, rows] = column_sum(total.T)
         for i in range(3):
             hsum_ref[:, i : i + 1] = jnp.sum(ghead[i], axis=1, keepdims=True)
 
@@ -700,7 +697,7 @@
         [
             pairs_out(channels + heads, LOW),
             fixed_out((8, channels), F32),
-            fixed_out((channels, 8), F32),
+            fixed_out((8, channels), F32),
             fixed_out((heads, 8), F32),
         ],
         [
@@ -974,9 +971,9 @@
     small = jnp.concatenate(
         [
             jnp.sum(dnormed * h * r, axis=0),
-            csum[:, : taps + 1].T.reshape(-1),
+            csum[: taps + 1].reshape(-1),
             hsum[:, :3].T.reshape(-1),
-            gsum[:, 0],
+            gsum[0],
         ]
     )
     return g + dh, early, late, pending, small

time: 786 us -> 783 us (level)
  no operation moved by 1% of the time
where the time goes in v1:
time: 783 us; the launch traced here: 776 us
  Pallas kernels  234 us (30%)
  matrix products  177 us (23%)
  waiting for transfers between devices  132 us (17%)
  other arithmetic  84.1 us (11%)
  starting transfers between devices  79.3 us (10%)
  local copies, waits for them, and re-layouts  54.7 us (7%)
  between operations  15.2 us (2%)
    pallas_call x12, Pallas kernels, call(): pl.pallas_call(kernel, grid=grid, in_specs=[s for _, s in ins], out_specs...  224 us
    dot_general x32, matrix products, contract(): lax.dot_general(a, b, (((a_dim,), (b_dim,)), ((), ())), preferred_element...  177 us
    all_gather x3, waiting for transfers between devices, gathered(): everyone = lambda a: lax.all_gather(a, across, axis=0, tiled=True)  56.5 us
    ppermute x16, starting transfers between devices, shifted(): lax.ppermute(x, axis, [(i, i + by) for i in range(devices) if 0 <= i + by...  33.1 us
    ppermute x16, waiting for transfers between devices, shifted(): lax.ppermute(x, axis, [(i, i + by) for i in range(devices) if 0 <= i + by...  20.1 us
    ppermute x4, waiting for transfers between devices, summed(): value = value + lax.ppermute(value, axis, pairs)  19.8 us
    all_to_all x3, starting transfers between devices, over_head(): lax.all_to_all(part, 'head', split_axis=0, concat_axis=0, tiled=True)  19.2 us
  transfers between devices with their start and end apart: 41, of which 15 were waited for; matrix products, arithmetic and copies ran while one was open for 33% of the time, Pallas kernels for 28%

profile of v1, /device:TPU:0, one launch (start us, length us, event | category | flops | bytes accessed | tf_op | source)
XLA Modules:
  0.0 775.7 jit_solution(4416421328159573372)
XLA Ops:
  13.5 6.9 bitcast_select_fusion.1
  21.1 6.4 collective-permute-done.2
  31.6 7.5 multiply_reduce_fusion.5
  46.3 4.8 collective-permute-start.3
  59.3 56.5 %all-gather.4.cloned.1.call-done = bf16[1024,6432]{1,0:T(8,128)(2,1)} async-done(((bf16[32,6432]{1,0:T(8,128)(2,1)}), bf16[1024,6432]{1,0:T(8,128)(2,1)}) %all-gather.4.cloned.1.call-update) | async-done | bytes 13172752 | tf_op jit(solution)/shard_map/all_gather | solution.py:819
  115.7 12.4 %convolution_convert_fusion.1.u_ref.halo_ref.step_ref = bf16[2336,1152]{1,0:T(8,128)(2,1)} fusion(bf16[1024,6432]{1,0:T(8,128)(2,1)} %all-gather.4.cloned.1.call-done, bf16[8,1024]{1,0:T(8,128)(2,1)S(1)} %multiply_convert_fusion.3, bf16[1024,1024]{1,0:T(8,128)(2,1)} %multiply_convert_fusion.1, bf16[1152]{0:T(1024)(128)(2,1)S(1)} %pad.24.clone), kind=kOutput, calls=%fused_computation.1 | convolution fusion | flops 5521084416 | bytes 12478720 | tf_op jit(solution)/shard_map/dot_general | solution.py:22
  128.2 17.1 %shard_map.177 = (bf16[2048,1024]{1,0:T(8,128)(2,1)}, bf16[2304,1024]{1,0:T(8,128)(2,1)}, bf16[256,1024]{1,0:T(8,128)(2,1)}, f32[32,1024]{1,0:T(8,128)}, f32[32,...) custom-call(bf16[2336,1152]{1,0:T(8,128)(2,1)} %convolution_convert_, ...), custom_call_target="tpu_custom_call" | custom-call | flops 536870912 | bytes 18874368 | tf_op jit(solution)/shard_map/pallas_call | solution.py:68
  145.3 4.2 collective-permute-start.6
  153.1 8.5 %convolution_convert_fusion.5.z_ref = bf16[2048,1024]{1,0:T(8,128)(2,1)} fusion(bf16[1024,1024]{1,0:T(8,128)(2,1)S(1)} %copy-done.18, bf16[1024,6432]{1,0:T(8,128)(2,1)} %all-gather.4.cloned.1.call-done), kind=kOutput, calls=%fused_computation.39 | convolution fusion | flops 4297064448 | bytes 10485760 | tf_op jit(solution)/shard_map/dot_general | solution.py:22
  161.6 11.9 %shard_map.178.yl_ref = bf16[2048,1024]{1,0:T(8,128)(2,1)} custom-call(bf16[2048,1024]{1,0:T(8,128)(2,1)} %get-tuple-element.90.xs_ref, bf16[256,1024]{1,0:T(8,128)(2,1)} %get-tuple-element.91.bc_ref, f32[32,1024]{1,0:T(8,128)} %get-tuple-element.92.dt_ref, f32[32,1024]{1,0:T(8,128)} %get-tuple-element.93.w_ref, f32[1024,32]{1,0:T(8,128)} %get-tuple-element.94.wcol_ref, ...), custom_call_target="tpu_custom_call" | custom-call | flops 2684354560 | bytes 12582912 | tf_op jit(solution)/shard_map/pallas_call | solution.py:68
  173.5 7.1 collective-permute-done.5
  183.5 14.7 %shard_map.179 = (bf16[2048,1024]{1,0:T(8,128)(2,1)}, bf16[2,1024,1024]{2,1,0:T(8,128)(2,1)}, bf16[2,2,512,1024]{3,2,1,0:T(8,128)(2,1)}) custom-call(bf16[2048,1024]{1,0:T(8,128)(2,1)} %shard_map.178.yl_ref, bf16[2048,1024]{1,0:T(8,128)(2,1)} %get-tuple-element.90.xs_ref, bf16[2048,1024]{1,0:T(8,128)(2,1)} %convolution_convert_fusion.5.z_ref, ...), custom_call_target="tpu_custom_call" | custom-call | flops 536870912 | bytes 29360128 | tf_op jit(solution)/shard_map/pallas_call | solution.py:68
  198.2 4.9 fusion.26
  203.1 4.6 multiply_reduce_fusion.4
  207.8 4.6 collective-permute-start.7
  212.9 8.6 %convolution_convert_fusion.4.z_ref = bf16[2048,1024]{1,0:T(8,128)(2,1)} fusion(bf16[1024,1024]{1,0:T(8,128)(2,1)S(1)} %multiply_convert_fusion, bf16[1024,4384]{1,0:T(8,128)(2,1)} %all-gather.6.cloned.1.call-done), kind=kOutput, calls=%fused_computation.38 | convolution fusion | flops 4297064448 | bytes 10485760 | tf_op jit(solution)/shard_map/dot_general | solution.py:22
  222.1 8.8 %convolution_convert_fusion.u_ref.halo_ref.step_ref = bf16[2336,1152]{1,0:T(8,128)(2,1)} fusion(bf16[1152,1024]{1,0:T(8,128)(2,1)S(1)} %pad_maximum_fusion.2, bf16[1024,4384]{1,0:T(8,128)(2,1)S(1)} %copy-done.50), kind=kOutput, calls=%fused_computation | convolution fusion | flops 5514006528 | bytes 12722176 | tf_op jit(solution)/shard_map/dot_general | solution.py:22
  230.9 17.2 %shard_map.180 = (bf16[2048,1024]{1,0:T(8,128)(2,1)}, bf16[2304,1024]{1,0:T(8,128)(2,1)}, bf16[256,1024]{1,0:T(8,128)(2,1)}, f32[32,1024]{1,0:T(8,128)}, f32[32,...) custom-call(bf16[2336,1152]{1,0:T(8,128)(2,1)} %convolution_convert_, ...), custom_call_target="tpu_custom_call" | custom-call | flops 536870912 | bytes 18874368 | tf_op jit(solution)/shard_map/pallas_call | solution.py:68
  261.6 11.6 %shard_map.181.yl_ref = bf16[2048,1024]{1,0:T(8,128)(2,1)} custom-call(bf16[2048,1024]{1,0:T(8,128)(2,1)} %get-tuple-element.103.xs_ref, bf16[256,1024]{1,0:T(8,128)(2,1)} %get-tuple-element.104.bc_ref, f32[32,1024]{1,0:T(8,128)} %get-tuple-element.105.dt_ref, f32[32,1024]{1,0:T(8,128)} %get-tuple-element.106.w_ref, f32[1024,32]{1,0:T(8,128)} %get-tuple-element.107.wcol_ref, ...), custom_call_target="tpu_custom_call" | custom-call | flops 2684354560 | bytes 12582912 | tf_op jit(solution)/shard_map/pallas_call | solution.py:68
  273.2 7.6 collective-permute-done.9
  283.7 14.8 %shard_map.182 = (bf16[2048,1024]{1,0:T(8,128)(2,1)}, bf16[2,1024,1024]{2,1,0:T(8,128)(2,1)}, bf16[2,2,512,1024]{3,2,1,0:T(8,128)(2,1)}) custom-call(bf16[2048,1024]{1,0:T(8,128)(2,1)} %shard_map.181.yl_ref, bf16[2048,1024]{1,0:T(8,128)(2,1)} %get-tuple-element.103.xs_ref, bf16[2048,1024]{1,0:T(8,128)(2,1)} %convolution_convert_fusion.4.z_ref, ...), custom_call_target="tpu_custom_call" | custom-call | flops 536870912 | bytes 29360128 | tf_op jit(solution)/shard_map/pallas_call | solution.py:68
  298.5 4.2 fusion.123
  302.7 5.4 fusion.20
  309.4 4.7 add_add_fusion
  319.1 3.7 convolution_convert_fusion.10.dg1_ref
  326.5 17.1 %shard_map.183 = (bf16[2048,1024]{1,0:T(8,128)(2,1)}, bf16[2048,1024]{1,0:T(8,128)(2,1)}, f32[8,2048]{1,0:T(8,128)}, bf16[2080,128]{1,0:T(8,128)(2,1)}) custom-call(bf16[1024,1024]{1,0:T(8,128)(2,1)} %convolution_convert_fusion.11.dg0_ref, bf16[1024,1024]{1,0:T(8,128)(2,1)} %convolution_convert_fusion.10.dg1_ref, ...), custom_call_target="tpu_custom_call" | custom-call | tf_op jit(solution)/shard_map/pallas_call | solution.py:68
  343.7 4.6 convolution_convert_fusion.7
  359.7 17.4 %shard_map.184 = (bf16[2048,1024]{1,0:T(8,128)(2,1)}, f32[32,1024]{1,0:T(8,128)}, f32[256,1024]{1,0:T(8,128)}) custom-call(bf16[2048,1024]{1,0:T(8,128)(2,1)} %get-tuple-element.103.xs_ref, bf16[2048,1024]{1,0:T(8,128)(2,1)} %get-tuple-element.122.dy_ref, bf16[256,1024]{1,0:T(8,128)(2,1)} %get-tuple-element.104.bc_ref, ...), custom_call_target="tpu_custom_call" | custom-call | flops 6442450944 | bytes 12582912 | tf_op jit(solution)/shard_map/pallas_call | solution.py:68
  377.2 4.4 fusion.68
  385.3 7.1 fusion
  392.4 34.3 %shard_map.185 = (bf16[2336,1024]{1,0:T(8,128)(2,1)}, f32[8,2304]{1,0:T(8,128)}, f32[8,2304]{1,0:T(8,128)}, f32[32,8]{1,0:T(8,128)}) custom-call(bf16[2336,1152]{1,0:T(8,128)(2,1)} %convolution_convert_fusion.u_ref.halo_ref.step_ref, bf16[2336,1152]{1,0:T(8,128)(2,1)} %convolution_convert_fusion.u_ref.halo_ref.step_ref, ...), custom_call_target="tpu_custom_call" | custom-call | flops 2684354560 | bytes 38797312 | tf_op jit(solution)/shard_map/pallas_call | solution.py:68
  428.0 8.6 %fusion.10 = f32[1024,1024]{1,0:T(8,128)} fusion(bf16[2048,1024]{1,0:T(8,128)(2,1)S(1)} %copy-done.55, bf16[1024,4384]{1,0:T(8,128)(2,1)} %all-gather.6.cloned.1.call-done), kind=kOutput, calls=%fused_computation.40 | convolution fusion | flops 4294967296 | bytes 12582912 | tf_op jit(solution)/shard_map/dot_general | solution.py:22
  437.3 4.9 shard_map.186
  442.2 5.5 convolution_convert_fusion.3
  458.0 6.7 all-to-all-start
  464.8 11.8 %multiply_reduce_fusion = (f32[1024]{0:T(1024)S(1)}, f32[1024]{0:T(1024)S(1)}, f32[1024,1024]{1,0:T(8,128)S(1)}) fusion(f32[1024,1024]{1,0:T(8,128)} %copy-done.2, f32[1024]{0:T(1024)S(1)} %add_rsqrt_fusion, f32[1024]{0:T(1024)S(1)} %slice.354, f32[1024,1024]{1,0:T(8,128)} %fusion.10, bf16[2336,1024]{1,0:T(8,128)(2,1)} %shard_map.186, ...), kind=kOutput, calls=%fused_computation.24 | convolution fusion | flops 4906285056 | bytes 22364160 | tf_op jit(solution)/shard_map/dot_general | solution.py:22
  479.2 13.3 %reduce-scatter.2.cloned.1.call-done = bf16[32,4096]{1,0:T(8,128)(2,1)} async-done(((bf16[512,4096]{1,0:T(8,128)(2,1)}), bf16[32,4096]{1,0:T(8,128)(2,1)}) %reduce-scatter.2.cloned.1.call-update) | async-done | bytes 262160 | tf_op jit(solution)/shard_map/reduce_scatter | solution.py:872
  497.0 5.3 convolution_convert_fusion.8.dg1_ref
  502.3 5.3 convolution_convert_fusion.9.dg0_ref
  507.6 16.7 %shard_map.187 = (bf16[2048,1024]{1,0:T(8,128)(2,1)}, bf16[2048,1024]{1,0:T(8,128)(2,1)}, f32[8,2048]{1,0:T(8,128)}, bf16[2080,128]{1,0:T(8,128)(2,1)}) custom-call(bf16[1024,1024]{1,0:T(8,128)(2,1)} %convolution_convert_fusion.9.dg0_ref, bf16[1024,1024]{1,0:T(8,128)(2,1)} %convolution_convert_fusion.8.dg1_ref, ...), custom_call_target="tpu_custom_call" | custom-call | tf_op jit(solution)/shard_map/pallas_call | solution.py:68
  524.4 4.7 convolution_convert_fusion.6
  544.5 17.3 %shard_map.188 = (bf16[2048,1024]{1,0:T(8,128)(2,1)}, f32[32,1024]{1,0:T(8,128)}, f32[256,1024]{1,0:T(8,128)}) custom-call(bf16[2048,1024]{1,0:T(8,128)(2,1)} %get-tuple-element.90.xs_ref, bf16[2048,1024]{1,0:T(8,128)(2,1)} %get-tuple-element.143.dy_ref, bf16[256,1024]{1,0:T(8,128)(2,1)} %get-tuple-element.91.bc_ref, f32[32,1024]{1,0:T(8,128)} %get-tuple-element.92.dt_ref, ...), custom_call_target="tpu_custom_call" | custom-call | flops 6442450944 | bytes 12582912 | tf_op jit(solution)/shard_map/pallas_call | solution.py:68
  562.7 3.8 fusion.59
  570.1 4.4 fusion.57
  579.0 6.0 fusion.1
  585.0 7.8 %all-to-all-start.2 = ((bf16[4,128,4096]{2,1,0:T(8,128)(2,1)}), bf16[4,128,4096]{2,1,0:T(8,128)(2,1)}, u32[]{:S(2)}, u32[]{:S(2)}) async-start(bf16[4,128,4096]{2,1,0:T(8,128)(2,1)} %bitcast.195), calls=%async_computation.3 | async-start | bytes 8388608 | tf_op jit(solution)/shard_map/all_to_all | solution.py:860
  592.8 34.1 %shard_map.189 = (bf16[2336,1024]{1,0:T(8,128)(2,1)}, f32[8,2304]{1,0:T(8,128)}, f32[8,2304]{1,0:T(8,128)}, f32[32,8]{1,0:T(8,128)}) custom-call(bf16[2336,1152]{1,0:T(8,128)(2,1)} %convolution_convert_fusion.1.u_ref.halo_ref.step_ref, bf16[2336,1152]{1,0:T(8,128)(2,1)} %convolution_convert_fusion.1.u_ref.halo_ref.step_ref, ...), custom_call_target="tpu_custom_call" | custom-call | flops 2684354560 | bytes 38797312 | tf_op jit(solution)/shard_map/pallas_call | solution.py:68
  627.0 8.8 %fusion.13 = f32[1024,1024]{1,0:T(8,128)} fusion(bf16[2048,1024]{1,0:T(8,128)(2,1)S(1)} %copy-done.53, bf16[1024,6432]{1,0:T(8,128)(2,1)} %all-gather.4.cloned.1.call-done), kind=kOutput, calls=%fused_computation.43 | convolution fusion | flops 4294967296 | bytes 12582912 | tf_op jit(solution)/shard_map/dot_general | solution.py:22
  635.7 4.7 all-to-all-done.2
  640.5 4.2 reduce_sum.150
  644.7 4.8 all-to-all-start.3
  650.8 5.4 collective-permute-done.21.ahead_ref
  656.8 4.8 shard_map.190
  661.6 6.4 convolution_convert_fusion.2
  668.1 5.9 all-to-all-done.3
  674.2 4.3 collective-permute-start.23
  680.7 6.1 fusion.3
  688.7 4.7 all-to-all-start.4
  693.4 12.8 %multiply_reduce_fusion.1 = (f32[1024]{0:T(1024)S(1)}, f32[1024]{0:T(1024)S(1)}, f32[1024,1024]{1,0:T(8,128)}) fusion(f32[1024,1024]{1,0:T(8,128)} %copy-done, f32[1024]{0:T(1024)S(1)} %copy-done.36, f32[1024]{0:T(1024)S(1)} %copy-done.30, f32[1024,1024]{1,0:T(8,128)} %fusion.13, bf16[2336,1024]{1,0:T(8,128)(2,1)} %shard_map.190, ...), kind=kOutput, calls=%fused_computation.25 | convolution fusion | flops 4906285056 | bytes 22364160 | tf_op jit(solution)/shard_map/dot_general | solution.py:22
  710.0 12.3 %collective-permute-done.26 = f32[14688]{0:T(1024)S(1)} collective-permute-done((f32[14688]{0:T(1024)S(1)}, f32[14688]{0:T(1024)S(1)}, u32[]{:S(2)}, u32[]{:S(2)}) %collective-permute-start.26) | collective-permute-done | bytes 58784 | tf_op jit(solution)/shard_map/ppermute | solution.py:779
  726.7 4.2 collective-permute-done.28
  736.0 4.2 all-to-all-start.5
  740.2 7.8 %select_bitcast_fusion.1 = (f32[1,1024,1024]{2,1,0:T(8,128)}, f32[1024,1024]{1,0:T(8,128)}) fusion(f32[1024,1024]{1,0:T(8,128)} %collective-permute-done.23, pred[]{:T(512)S(6)} %eq.4, f32[1024,1024]{1,0:T(8,128)} %get-tuple-element.225, f32[1024,1024]{1,0:T(8,128)} %copy-done, f32[1024]{0:T(1024)S(1)} %fusion.101, f32[1024,1024]{1,0:T(8,128)} %get-tuple-element.261, ...), kind=kLoop, calls=%fused_computation.27 | loop fusion | flops 6291456 | bytes 25178112 | tf_op jit(solution)/shard_map/stack | solution.py:1058
  764.7 4.2 maximum_bitcast_fusion
  (334 shorter events, 155.2 us)
Async XLA Ops:
  7.2 108.6 %all-gather.4.cloned.1.call-start = ((), (), s32[]{:S(2)}) async-start(), calls=%async_computation.7 | async-start | bytes 13787136 | tf_op jit(solution)/shard_map/all_gather | solution.py:819
  9.7 1.9 collective-permute-start.1
  12.5 200.3 %all-gather.6.cloned.1.call-start = ((), (), s32[]{:S(2)}) async-start(), calls=%async_computation.8 | async-start | bytes 9461760 | tf_op jit(solution)/shard_map/all_gather | solution.py:819
  13.4 289.3 %all-gather.8.cloned.1.call-start = ((), (), s32[]{:S(2)}) async-start(), calls=%async_computation.9 | async-start | bytes 4325376 | tf_op jit(solution)/shard_map/all_gather | solution.py:819
  20.3 11.2 %collective-permute-start = (f32[1024,1024]{1,0:T(8,128)}, f32[1024,1024]{1,0:T(8,128)}, u32[]{:S(2)}, u32[]{:S(2)}) collective-permute-start(f32[1024,1024]{1,0:T(8,128)} %bitcast_select_fusion.1), channel_id=1, source_target_pairs={{0,16},{16,0},{1,17},{17,1},{2,18},{18,2},{3,19},{19,3},{4,20},{20... | collective-permute-start | bytes 12582920 | tf_op jit(solution)/shard_map/ppermute | solution.py:767
  20.9 6.5 collective-permute-start.2
  27.6 31.6 %copy-start.29 = (f32[1024]{0:T(1024)}, f32[1024]{0:T(1024)S(1)}, u32[]{:S(2)}) copy-start(f32[1024]{0:T(1024)S(1)} %slice.337) | copy-start | bytes 12292
  39.0 13.9 %copy-start = (f32[1024,1024]{1,0:T(8,128)}, f32[1024,1024]{1,0:T(8,128)S(1)}, u32[]{:S(2)}) copy-start(f32[1024,1024]{1,0:T(8,128)S(1)} %get-tuple-element.227) | copy-start | bytes 12582916
  39.0 13.9 %copy-start.37 = (f32[1024]{0:T(1024)}, f32[1024]{0:T(1024)S(1)}, u32[]{:S(2)}) copy-start(f32[1024]{0:T(1024)S(1)} %get-tuple-element.226) | copy-start | bytes 12292
  46.3 12.7 %collective-permute-start.3 = (f32[8,1024]{1,0:T(8,128)S(1)}, f32[8,1024]{1,0:T(8,128)S(1)}, u32[]{:S(2)}, u32[]{:S(2)}) collective-permute-start(f32[8,1024]{1,0:T(8,128)S(1)} %slice.338), channel_id=1, source_target_pairs={{0,1},{1,2},{2,3},{4,5},{5,6},{6,7},{8,9},{9,10},{10,11},{12,13},{... | collective-permute-start | bytes 98312 | tf_op jit(solution)/shard_map/ppermute | solution.py:761
  128.2 24.9 %copy-start.18 = (bf16[1024,1024]{1,0:T(8,128)(2,1)S(1)}, bf16[1024,1024]{1,0:T(8,128)(2,1)}, u32[]{:S(2)}) copy-start(bf16[1024,1024]{1,0:T(8,128)(2,1)} %multiply_convert_fusion.1) | copy-start | bytes 6291460
  145.3 28.2 %collective-permute-start.6 = (bf16[2080,128]{1,0:T(8,128)(2,1)}, bf16[2080,128]{1,0:T(8,128)(2,1)}, u32[]{:S(2)}, u32[]{:S(2)}) collective-permute-start(bf16[2080,128]{1,0:T(8,128)(2,1)} %get-tuple-element.97), channel_id=1, source_target_pairs={{0,3},{4,7},{8,11},{12,15},{16,19},{20,23},{24,27},{28,31}} | collective-permute-start | bytes 1597448 | tf_op jit(solution)/shard_map/ppermute | solution.py:761
  149.4 31.1 %collective-permute-start.5 = (bf16[2080,128]{1,0:T(8,128)(2,1)}, bf16[2080,128]{1,0:T(8,128)(2,1)S(1)}, u32[]{:S(2)}, u32[]{:S(2)}) collective-permute-start(bf16[2080,128]{1,0:T(8,128)(2,1)} %get-tuple-element.97), channel_id=1, source_target_pairs={{0,2},{1,3},{4,6},{5,7},{8,10},{9,11},{12,14},{13,15},{16,18},{17,... | collective-permute-start | bytes 1597448 | tf_op jit(solution)/shard_map/ppermute | solution.py:761
  150.8 29.8 %collective-permute-start.4 = (bf16[2080,128]{1,0:T(8,128)(2,1)}, bf16[2080,128]{1,0:T(8,128)(2,1)S(1)}, u32[]{:S(2)}, u32[]{:S(2)}) collective-permute-start(bf16[2080,128]{1,0:T(8,128)(2,1)} %get-tuple-element.97), channel_id=1, source_target_pairs={{0,1},{1,2},{2,3},{4,5},{5,6},{6,7},{8,9},{9,10},{10,11},{12,13},{... | collective-permute-start | bytes 1597448 | tf_op jit(solution)/shard_map/ppermute | solution.py:761
  152.5 340.0 %reduce-scatter.2.cloned.1.call-start = ((), (), s32[]{:S(2)}) async-start(), calls=%async_computation.10 | async-start | bytes 4456448 | tf_op jit(solution)/shard_map/reduce_scatter | solution.py:872
  207.8 13.7 %copy-start.40 = (f32[1024]{0:T(1024)}, f32[1024]{0:T(1024)S(1)}, u32[]{:S(2)}) copy-start(f32[1024]{0:T(1024)S(1)} %get-tuple-element.258) | copy-start | bytes 12292
  207.8 13.7 %collective-permute-start.7 = (f32[8,1024]{1,0:T(8,128)S(1)}, f32[8,1024]{1,0:T(8,128)S(1)}, u32[]{:S(2)}, u32[]{:S(2)}) collective-permute-start(f32[8,1024]{1,0:T(8,128)S(1)} %slice.355), channel_id=1, source_target_pairs={{0,1},{1,2},{2,3},{4,5},{5,6},{6,7},{8,9},{9,10},{10,11},{12,13},{... | collective-permute-start | bytes 98312 | tf_op jit(solution)/shard_map/ppermute | solution.py:761
  230.9 23.3 %copy-start.3 = (f32[1024,1024]{1,0:T(8,128)S(1)}, f32[1024,1024]{1,0:T(8,128)}, u32[]{:S(2)}) copy-start(f32[1024,1024]{1,0:T(8,128)} %copy-done.2) | copy-start | bytes 12582916
  248.1 25.1 %collective-permute-start.10 = (bf16[2080,128]{1,0:T(8,128)(2,1)}, bf16[2080,128]{1,0:T(8,128)(2,1)}, u32[]{:S(2)}, u32[]{:S(2)}) collective-permute-start(bf16[2080,128]{1,0:T(8,128)(2,1)} %get-tuple-element.110), channel_id=1, source_target_pairs={{0,3},{4,7},{8,11},{12,15},{16,19},{20,23},{24,27},{28,31}} | collective-permute-start | bytes 1597448 | tf_op jit(solution)/shard_map/ppermute | solution.py:761
  250.2 30.6 %collective-permute-start.9 = (bf16[2080,128]{1,0:T(8,128)(2,1)}, bf16[2080,128]{1,0:T(8,128)(2,1)S(1)}, u32[]{:S(2)}, u32[]{:S(2)}) collective-permute-start(bf16[2080,128]{1,0:T(8,128)(2,1)} %get-tuple-element.110), channel_id=1, source_target_pairs={{0,2},{1,3},{4,6},{5,7},{8,10},{9,11},{12,14},{13,15},{16,18},{17,... | collective-permute-start | bytes 1597448 | tf_op jit(solution)/shard_map/ppermute | solution.py:761
  251.5 29.3 %collective-permute-start.8 = (bf16[2080,128]{1,0:T(8,128)(2,1)}, bf16[2080,128]{1,0:T(8,128)(2,1)S(1)}, u32[]{:S(2)}, u32[]{:S(2)}) collective-permute-start(bf16[2080,128]{1,0:T(8,128)(2,1)} %get-tuple-element.110), channel_id=1, source_target_pairs={{0,1},{1,2},{2,3},{4,5},{5,6},{6,7},{8,9},{9,10},{10,11},{12,13},{... | collective-permute-start | bytes 1597448 | tf_op jit(solution)/shard_map/ppermute | solution.py:761
  302.7 14.2 %copy-start.21 = (bf16[2,1,512,1024]{3,2,1,0:T(8,128)(2,1)}, bf16[2,1,512,1024]{3,2,1,0:T(8,128)(2,1)S(1)}, u32[]{:S(2)}) copy-start(bf16[2,1,512,1024]{3,2,1,0:T(8,128)(2,1)S(1)} %get-tuple-element.232) | copy-start | bytes 6291460
  326.5 17.1 %copy-start.17 = (bf16[2,1,4,4,32,1024]{5,4,3,2,0,1:T(8,128)(2,1)S(1)}, bf16[2,1,4,4,32,1024]{5,4,3,2,0,1:T(8,128)(2,1)}, u32[]{:S(2)}) copy-start(bf16[2,1,4,4,32,1024]{5,4,3,2,0,1:T(8,128)(2,1)} %copy.84) | copy-start | bytes 6291460
  350.5 34.8 %collective-permute-start.11 = (bf16[512,4096]{1,0:T(8,128)(2,1)}, bf16[512,4096]{1,0:T(8,128)(2,1)}, u32[]{:S(2)}, u32[]{:S(2)}) collective-permute-start(bf16[512,4096]{1,0:T(8,128)(2,1)} %pad_maximum_fusion), channel_id=1, source_target_pairs={{0,16},{16,0},{1,17},{17,1},{2,18},{18,2},{3,19},{19,3},{4,20},{20... | collective-permute-start | bytes 12582920 | tf_op jit(solution)/shard_map/ppermute | solution.py:767
  350.5 31.0 %collective-permute-start.14 = (bf16[2080,128]{1,0:T(8,128)(2,1)}, bf16[2080,128]{1,0:T(8,128)(2,1)S(1)}, u32[]{:S(2)}, u32[]{:S(2)}) collective-permute-start(bf16[2080,128]{1,0:T(8,128)(2,1)} %get-tuple-element.127), channel_id=1, source_target_pairs={{3,0},{7,4},{11,8},{15,12},{19,16},{23,20},{27,24},{31,28}} | collective-permute-start | bytes 1597448 | tf_op jit(solution)/shard_map/ppermute | solution.py:761
  351.9 29.6 %collective-permute-start.13 = (bf16[2080,128]{1,0:T(8,128)(2,1)}, bf16[2080,128]{1,0:T(8,128)(2,1)S(1)}, u32[]{:S(2)}, u32[]{:S(2)}) collective-permute-start(bf16[2080,128]{1,0:T(8,128)(2,1)} %get-tuple-element.127), channel_id=1, source_target_pairs={{2,0},{3,1},{6,4},{7,5},{10,8},{11,9},{14,12},{15,13},{18,16},{19,... | collective-permute-start | bytes 1597448 | tf_op jit(solution)/shard_map/ppermute | solution.py:761
  353.2 28.3 %collective-permute-start.12 = (bf16[2080,128]{1,0:T(8,128)(2,1)}, bf16[2080,128]{1,0:T(8,128)(2,1)S(1)}, u32[]{:S(2)}, u32[]{:S(2)}) collective-permute-start(bf16[2080,128]{1,0:T(8,128)(2,1)} %get-tuple-element.127), channel_id=1, source_target_pairs={{1,0},{2,1},{3,2},{5,4},{6,5},{7,6},{9,8},{10,9},{11,10},{13,12},{... | collective-permute-start | bytes 1597448 | tf_op jit(solution)/shard_map/ppermute | solution.py:761
  359.7 17.4 %copy-start.54 = (bf16[2048,1024]{1,0:T(8,128)(2,1)S(1)}, bf16[2048,1024]{1,0:T(8,128)(2,1)}, u32[]{:S(2)}) copy-start(bf16[2048,1024]{1,0:T(8,128)(2,1)} %get-tuple-element.132) | copy-start | bytes 12582916
  392.4 35.6 %copy-start.55 = (bf16[2048,1024]{1,0:T(8,128)(2,1)S(1)}, bf16[2048,1024]{1,0:T(8,128)(2,1)}, u32[]{:S(2)}) copy-start(bf16[2048,1024]{1,0:T(8,128)(2,1)} %get-tuple-element.132) | copy-start | bytes 12582916
  426.7 10.0 %collective-permute-start.15 = (f32[8,2304]{1,0:T(8,128)}, f32[8,2304]{1,0:T(8,128)S(1)}, u32[]{:S(2)}, u32[]{:S(2)}) collective-permute-start(f32[8,2304]{1,0:T(8,128)} %get-tuple-element.131), channel_id=1, source_target_pairs={{1,0},{2,1},{3,2},{5,4},{6,5},{7,6},{9,8},{10,9},{11,10},{13,12},{... | collective-permute-start | bytes 221192 | tf_op jit(solution)/shard_map/ppermute | solution.py:761
  447.6 4.6 collective-permute-start.16
  458.0 74.7 %all-to-all-start = ((bf16[4,128,2336]{1,2,0:T(8,128)(2,1)}), bf16[4,128,2336]{1,2,0:T(8,128)(2,1)}, u32[]{:S(2)}, u32[]{:S(2)}) async-start(bf16[4,128,2336]{1,2,0:T(8,128)(2,1)} %copy_bitcast_fusion.1), calls=%async_computation.1 | async-start | bytes 4784128 | tf_op jit(solution)/shard_map/all_to_all | solution.py:860
  464.8 11.8 %copy-start.5 = (f32[1024,1024]{1,0:T(8,128)S(1)}, f32[1024,1024]{1,0:T(8,128)}, u32[]{:S(2)}) copy-start(f32[1024,1024]{1,0:T(8,128)} %copy-done.2) | copy-start | bytes 12582916
  464.8 11.8 %copy-start.7 = (f32[1024,1024]{1,0:T(8,128)S(1)}, f32[1024,1024]{1,0:T(8,128)}, u32[]{:S(2)}) copy-start(f32[1024,1024]{1,0:T(8,128)} %get-tuple-element.116) | copy-start | bytes 12582916
  479.2 49.9 %copy-start.12 = (bf16[1024,1024]{1,0:T(8,128)(2,1)}, bf16[1024,1024]{1,0:T(8,128)(2,1)S(1)}, u32[]{:S(2)}) copy-start(bf16[1024,1024]{1,0:T(8,128)(2,1)S(1)} %get-tuple-element.136) | copy-start | bytes 6291460
  507.6 16.7 %copy-start.14 = (bf16[2,1,4,4,32,1024]{5,4,3,2,0,1:T(8,128)(2,1)S(1)}, bf16[2,1,4,4,32,1024]{5,4,3,2,0,1:T(8,128)(2,1)}, u32[]{:S(2)}) copy-start(bf16[2,1,4,4,32,1024]{5,4,3,2,0,1:T(8,128)(2,1)} %copy.82) | copy-start | bytes 6291460
  532.7 46.4 %collective-permute-start.17 = (bf16[512,4096]{1,0:T(8,128)(2,1)}, bf16[512,4096]{1,0:T(8,128)(2,1)}, u32[]{:S(2)}, u32[]{:S(2)}) collective-permute-start(bf16[512,4096]{1,0:T(8,128)(2,1)} %pad_maximum_fusion.1), channel_id=1, source_target_pairs={{0,16},{16,0},{1,17},{17,1},{2,18},{18,2},{3,19},{19,3},{4,20},{20... | collective-permute-start | bytes 12582920 | tf_op jit(solution)/shard_map/ppermute | solution.py:767
  537.1 24.7 %all-to-all-start.1 = ((bf16[4,32,2336]{2,1,0:T(8,128)(2,1)}), bf16[4,32,2336]{2,1,0:T(8,128)(2,1)S(1)}, u32[]{:S(2)}, u32[]{:S(2)}) async-start(bf16[4,32,2336]{2,1,0:T(8,128)(2,1)} %bitcast.201), calls=%async_computation.2 | async-start | bytes 1245184 | tf_op jit(solution)/shard_map/all_to_all | solution.py:867
  540.6 33.8 %collective-permute-start.20 = (bf16[2080,128]{1,0:T(8,128)(2,1)}, bf16[2080,128]{1,0:T(8,128)(2,1)}, u32[]{:S(2)}, u32[]{:S(2)}) collective-permute-start(bf16[2080,128]{1,0:T(8,128)(2,1)} %get-tuple-element.148), channel_id=1, source_target_pairs={{3,0},{7,4},{11,8},{15,12},{19,16},{23,20},{27,24},{31,28}} | collective-permute-start | bytes 1597448 | tf_op jit(solution)/shard_map/ppermute | solution.py:761
  541.9 32.5 %collective-permute-start.19 = (bf16[2080,128]{1,0:T(8,128)(2,1)}, bf16[2080,128]{1,0:T(8,128)(2,1)}, u32[]{:S(2)}, u32[]{:S(2)}) collective-permute-start(bf16[2080,128]{1,0:T(8,128)(2,1)} %get-tuple-element.148), channel_id=1, source_target_pairs={{2,0},{3,1},{6,4},{7,5},{10,8},{11,9},{14,12},{15,13},{18,16},{19,... | collective-permute-start | bytes 1597448 | tf_op jit(solution)/shard_map/ppermute | solution.py:761
  543.2 31.2 %collective-permute-start.18 = (bf16[2080,128]{1,0:T(8,128)(2,1)}, bf16[2080,128]{1,0:T(8,128)(2,1)}, u32[]{:S(2)}, u32[]{:S(2)}) collective-permute-start(bf16[2080,128]{1,0:T(8,128)(2,1)} %get-tuple-element.148), channel_id=1, source_target_pairs={{1,0},{2,1},{3,2},{5,4},{6,5},{7,6},{9,8},{10,9},{11,10},{13,12},{... | collective-permute-start | bytes 1597448 | tf_op jit(solution)/shard_map/ppermute | solution.py:761
  544.5 18.2 %copy-start.13 = (bf16[1024,1024]{1,0:T(8,128)(2,1)S(1)}, bf16[1024,1024]{1,0:T(8,128)(2,1)}, u32[]{:S(2)}) copy-start(bf16[1024,1024]{1,0:T(8,128)(2,1)} %copy-done.12) | copy-start | bytes 6291460
  585.0 55.5 %all-to-all-start.2 = ((bf16[4,128,4096]{2,1,0:T(8,128)(2,1)}), bf16[4,128,4096]{2,1,0:T(8,128)(2,1)}, u32[]{:S(2)}, u32[]{:S(2)}) async-start(bf16[4,128,4096]{2,1,0:T(8,128)(2,1)} %bitcast.195), calls=%async_computation.3 | async-start | bytes 8388608 | tf_op jit(solution)/shard_map/all_to_all | solution.py:860
  592.8 34.1 %copy-start.53 = (bf16[2048,1024]{1,0:T(8,128)(2,1)S(1)}, bf16[2048,1024]{1,0:T(8,128)(2,1)}, u32[]{:S(2)}) copy-start(bf16[2048,1024]{1,0:T(8,128)(2,1)} %get-tuple-element.153) | copy-start | bytes 12582916
  635.7 13.7 %copy-start.58 = (f32[8,2304]{1,0:T(8,128)S(1)}, f32[8,2304]{1,0:T(8,128)}, u32[]{:S(2)}) copy-start(f32[8,2304]{1,0:T(8,128)} %get-tuple-element.152) | copy-start | bytes 221188
  644.7 29.3 %all-to-all-start.3 = ((bf16[4,32,4096]{2,1,0:T(8,128)(2,1)}), bf16[4,32,4096]{2,1,0:T(8,128)(2,1)S(1)}, u32[]{:S(2)}, u32[]{:S(2)}) async-start(bf16[4,32,4096]{2,1,0:T(8,128)(2,1)} %bitcast.46), calls=%async_computation.4 | async-start | bytes 2097152 | tf_op jit(solution)/shard_map/all_to_all | solution.py:867
  649.5 6.7 collective-permute-start.21
  661.6 17.8 %copy-start.33 = (f32[8,2304]{1,0:T(8,128)S(1)}, f32[8,2304]{1,0:T(8,128)}, u32[]{:S(2)}) copy-start(f32[8,2304]{1,0:T(8,128)} %get-tuple-element.164) | copy-start | bytes 221188
  661.6 17.8 %copy-start.42 = (f32[32,8]{1,0:T(8,128)S(1)}, f32[32,8]{1,0:T(8,128)}, u32[]{:S(2)}) copy-start(f32[32,8]{1,0:T(8,128)} %get-tuple-element.165) | copy-start | bytes 3076
  661.6 18.9 %copy-start.34 = (f32[8,2304]{1,0:T(8,128)S(1)}, f32[8,2304]{1,0:T(8,128)}, u32[]{:S(2)}) copy-start(f32[8,2304]{1,0:T(8,128)} %get-tuple-element.161) | copy-start | bytes 221188
  661.6 18.9 %copy-start.43 = (f32[32,8]{1,0:T(8,128)S(1)}, f32[32,8]{1,0:T(8,128)}, u32[]{:S(2)}) copy-start(f32[32,8]{1,0:T(8,128)} %get-tuple-element.162) | copy-start | bytes 3076
  674.1 6.6 collective-permute-start.22
  674.2 66.0 %collective-permute-start.23 = (f32[1024,1024]{1,0:T(8,128)}, f32[1024,1024]{1,0:T(8,128)}, u32[]{:S(2)}, u32[]{:S(2)}) collective-permute-start(f32[1024,1024]{1,0:T(8,128)} %add_add_fusion), channel_id=1, source_target_pairs={{0,16},{1,17},{2,18},{3,19},{4,20},{5,21},{6,22},{7,23},{8,24},{9,... | collective-permute-start | bytes 12582920 | tf_op jit(solution)/shard_map/ppermute | solution.py:1050
  688.7 42.8 %all-to-all-start.4 = ((bf16[4,128,2336]{1,2,0:T(8,128)(2,1)}), bf16[4,128,2336]{1,2,0:T(8,128)(2,1)}, u32[]{:S(2)}, u32[]{:S(2)}) async-start(bf16[4,128,2336]{1,2,0:T(8,128)(2,1)} %copy_bitcast_fusion), calls=%async_computation.5 | async-start | bytes 4784128 | tf_op jit(solution)/shard_map/all_to_all | solution.py:860
  693.4 33.3 %copy-start.38 = (f32[1024]{0:T(1024)S(1)}, f32[1024]{0:T(1024)}, u32[]{:S(2)}) copy-start(f32[1024]{0:T(1024)} %copy-done.37) | copy-start | bytes 12292
  706.3 1.3 collective-permute-start.25
  707.6 14.7 %collective-permute-start.26 = (f32[14688]{0:T(1024)S(1)}, f32[14688]{0:T(1024)S(1)}, u32[]{:S(2)}, u32[]{:S(2)}) collective-permute-start(f32[14688]{0:T(1024)S(1)} %select_add_fusion), channel_id=1, source_target_pairs={{0,1},{1,0},{2,3},{3,2},{4,5},{5,4},{6,7},{7,6},{8,9},{9,8},{10,11... | collective-permute-start | bytes 176264 | tf_op jit(solution)/shard_map/ppermute | solution.py:779
  722.3 4.3 collective-permute-start.27
  726.6 4.3 collective-permute-start.28
  731.5 17.7 %collective-permute-start.29 = (f32[14688]{0:T(1024)}, f32[14688]{0:T(1024)}, u32[]{:S(2)}, u32[]{:S(2)}) collective-permute-start(f32[14688]{0:T(1024)} %add.179), channel_id=1, source_target_pairs={{0,8},{4,12},{8,0},{12,4},{1,9},{5,13},{9,1},{13,5},{2,10},{6,14},... | collective-permute-start | bytes 176264 | tf_op jit(solution)/shard_map/ppermute | solution.py:779
  736.0 17.3 %all-to-all-start.5 = ((bf16[4,32,2336]{2,1,0:T(8,128)(2,1)}), bf16[4,32,2336]{2,1,0:T(8,128)(2,1)S(1)}, u32[]{:S(2)}, u32[]{:S(2)}) async-start(bf16[4,32,2336]{2,1,0:T(8,128)(2,1)} %bitcast.200), calls=%async_computation.6 | async-start | bytes 1245184 | tf_op jit(solution)/shard_map/all_to_all | solution.py:867
  740.1 13.2 %copy-start.11 = (f32[32,2336]{1,0:T(8,128)S(1)}, f32[32,2336]{1,0:T(8,128)}, u32[]{:S(2)}) copy-start(f32[32,2336]{1,0:T(8,128)} %convert_reduce_fusion.2) | copy-start | bytes 897028
  748.0 13.3 %collective-permute-start.24 = (f32[1024,1024]{1,0:T(8,128)}, f32[1024,1024]{1,0:T(8,128)}, u32[]{:S(2)}, u32[]{:S(2)}) collective-permute-start(f32[1024,1024]{1,0:T(8,128)} %get-tuple-element.223), channel_id=1, source_target_pairs={{16,0},{17,1},{18,2},{19,3},{20,4},{21,5},{22,6},{23,7},{24,8},{25... | collective-permute-start | bytes 12582920 | tf_op jit(solution)/shard_map/ppermute | solution.py:1056
  753.4 5.1 collective-permute-start.30
  (36 other events, 198.6 us)
Sparse Core Ops, SparseCore 0:
  12.7 103.0 all-gather.3
  118.6 81.7 all-gather.5
  203.2 72.7 all-gather.7
  392.5 99.9 reduce-scatter.1
